TPU v7x, 512 devices: a whole 4x4x16 slice. The times are simulated.
512 devices in a mesh: dp: 16 (over x, z_hi), pipe: 8 (over y, core), tensor: 4 (over z_lo).
Axes of the slice: x: 4, y: 4, z: 16 (z_hi: 4, z_lo: 4; z = z_hi * 4 + z_lo), core: 2. Of those that a mesh axis runs over, the one named last changes fastest.
Arguments:
- section_input: bfloat16 [8, 2048, 4096], P('pipe', 'dp'), may hold values from -60 to 60
- out_grad: bfloat16 [8, 2048, 4096], P('pipe', 'dp'), may hold values from -1 to 1
- head_grad: bfloat16 [8, 2048, 2048], P('pipe', 'dp', 'tensor'), may hold values from -8 to 8
- encoder: bfloat16 [2048, 4096], P(('dp', 'pipe', 'tensor')), may hold values from -12 to 12
- norm_gain: float32 [8, 4096], P('pipe'), may hold values from 0.25 to 1.75
- query_weight: bfloat16 [8, 4096, 2048], P('pipe', 'dp', 'tensor'), may hold values from -0.09375 to 0.09375
- key_weight: bfloat16 [8, 4096, 2048], P('pipe', 'dp', 'tensor'), may hold values from -0.09375 to 0.09375
- value_weight: bfloat16 [8, 4096, 2048], P('pipe', 'dp', 'tensor'), may hold values from -0.09375 to 0.09375
Outputs:
- input_grad: bfloat16 [8, 2048, 4096], P('pipe', 'dp', 'tensor')
- encoder_grad: float32 [2048, 4096], P(('dp', 'pipe', 'tensor'))
- gain_grad: float32 [8, 4096], P('pipe', 'tensor')
All inputs are finite; a program needn't handle non-finite values.
Results may differ from a plain program's by a relative error of at most 0.03.
Values may be sent and summed in bfloat16 or wider, within the bound.
A program may use at most 64 MiB of HBM per device.

v0:
```python
import math

import jax
import jax.numpy as jnp
from jax import lax
from jax.sharding import PartitionSpec as P

HEAD_DIM = 256


EPSILON = 1e-06


def contract_last(left, right):
    return lax.dot_general(
        left, right, (((1,), (1,)), ((), ())), preferred_element_type=jnp.float32
    )


def shards(
    section_input, out_grad, head_grad, encoder, norm_gain, query_weight, key_weight, value_weight
):
    model_width = section_input.shape[2]
    col_share = model_width // lax.axis_size("tensor")
    stream = section_input[0]
    upstream = out_grad[0]
    attn_grad = head_grad[0]
    gains = norm_gain[0]
    w_query, w_key, w_value = (
        lax.all_gather(query_weight[0], "dp", axis=0, tiled=True),
        lax.all_gather(key_weight[0], "dp", axis=0, tiled=True),
        lax.all_gather(value_weight[0], "dp", axis=0, tiled=True),
    )
    enc_full = lax.all_gather(encoder, ("pipe", "tensor"), axis=0, tiled=True)
    stream_f = stream.astype(jnp.float32)
    inv_rms = lax.rsqrt(jnp.mean(stream_f * stream_f, axis=-1, keepdims=True) + EPSILON)
    normed = stream_f * inv_rms
    hidden = (normed * gains).astype(jnp.bfloat16)
    queries = jnp.dot(hidden, w_query, preferred_element_type=jnp.float32).astype(jnp.bfloat16)
    keys_all = jnp.dot(enc_full, w_key, preferred_element_type=jnp.float32).astype(jnp.bfloat16)
    values_all = jnp.dot(enc_full, w_value, preferred_element_type=jnp.float32).astype(jnp.bfloat16)
    tgt_rows = queries.shape[0]
    src_rows = keys_all.shape[0]
    columns = queries.shape[1]
    heads_here = columns // HEAD_DIM
    head_scale = 1.0 / math.sqrt(HEAD_DIM)
    q_heads = queries.reshape(tgt_rows, heads_here, HEAD_DIM)
    k_heads = keys_all.reshape(src_rows, heads_here, HEAD_DIM)
    v_heads = values_all.reshape(src_rows, heads_here, HEAD_DIM)
    scores = (
        jnp.einsum("qhd,khd->hqk", q_heads, k_heads, preferred_element_type=jnp.float32)
        * head_scale
    )
    expo = jnp.exp(scores)
    probs = expo / jnp.sum(expo, axis=-1, keepdims=True)
    probs_low = probs.astype(jnp.bfloat16)
    a_heads = attn_grad.reshape(tgt_rows, heads_here, HEAD_DIM)
    prob_grad = jnp.einsum("qhd,khd->hqk", a_heads, v_heads, preferred_element_type=jnp.float32)
    score_grad = (
        probs * (prob_grad - jnp.sum(prob_grad * probs, axis=-1, keepdims=True)) * head_scale
    ).astype(jnp.bfloat16)
    query_grad = (
        jnp.einsum("hqk,khd->qhd", score_grad, k_heads, preferred_element_type=jnp.float32)
        .astype(jnp.bfloat16)
        .reshape(tgt_rows, columns)
    )
    key_grad = (
        jnp.einsum("hqk,qhd->khd", score_grad, q_heads, preferred_element_type=jnp.float32)
        .astype(jnp.bfloat16)
        .reshape(src_rows, columns)
    )
    value_grad = (
        jnp.einsum("hqk,qhd->khd", probs_low, a_heads, preferred_element_type=jnp.float32)
        .astype(jnp.bfloat16)
        .reshape(src_rows, columns)
    )
    hidden_part = contract_last(query_grad, w_query)
    offset = lax.axis_index("tensor") * col_share
    hidden_grad = lax.psum(hidden_part.astype(jnp.bfloat16), "tensor").astype(jnp.float32)
    normed_grad = hidden_grad * gains
    inner = jnp.mean(normed_grad * normed, axis=-1, keepdims=True)
    whole_grad = upstream.astype(jnp.float32) + inv_rms * (normed_grad - normed * inner)
    grad_in = lax.dynamic_slice_in_dim(whole_grad, offset, col_share, 1).astype(jnp.bfloat16)
    gain_part = lax.dynamic_slice_in_dim(
        jnp.sum(hidden_grad * normed, axis=0), offset, col_share, 0
    )
    gain_total = lax.psum(gain_part, "dp")
    enc_grad = lax.psum_scatter(
        (contract_last(key_grad, w_key) + contract_last(value_grad, w_value)).astype(jnp.bfloat16),
        ("pipe", "tensor"),
        scatter_dimension=0,
        tiled=True,
    ).astype(jnp.float32)
    return (grad_in[None], enc_grad, gain_total[None])


def solution(mesh):
    placed = (
        P("pipe", "dp", None),
        P("pipe", "dp", None),
        P("pipe", "dp", "tensor"),
        P(("dp", "pipe", "tensor"), None),
        P("pipe", None),
        P("pipe", "dp", "tensor"),
        P("pipe", "dp", "tensor"),
        P("pipe", "dp", "tensor"),
    )
    return jax.shard_map(
        shards,
        mesh=mesh,
        in_specs=placed,
        out_specs=(
            P("pipe", "dp", "tensor"),
            P(("dp", "pipe", "tensor"), None),
            P("pipe", "tensor"),
        ),
        check_vma=False,
    )
```

profile of v0, /device:TPU:24, one launch (start us, length us, event | category | flops | bytes accessed | tf_op | source)
XLA Modules:
  0.0 879.2 jit_solution(6146471033148001290)
XLA Ops:
  7.2 0.0 all-gather.15.cloned.1.call-start
  7.2 0.7 all-gather.15.cloned.1.call-update
  7.9 0.0 copy-start.1
  7.9 0.0 copy-start.2
  7.9 0.0 all-gather.11.cloned.1.call-start
  8.0 0.7 all-gather.11.cloned.1.call-update
  8.7 0.0 all-gather.9.cloned.1.call-start
  8.7 0.7 all-gather.9.cloned.1.call-update
  9.4 0.0 all-gather.13.cloned.1.call-start
  9.5 0.5 all-gather.13.cloned.1.call-update
  10.0 0.0 all-reduce.4.cloned.1.call-start
  10.0 0.9 reshape_squeeze.3
  11.0 1.5 fusion.13
  12.5 90.3 %all-gather.15.cloned.1.call-done = bf16[32,4,4096]{2,1,0:T(4,128)(2,1)} async-done(((bf16[1,4,4096]{2,1,0:T(4,128)(2,1)}), bf16[32,4,4096]{2,1,0:T(4,128)(2,1)}) %all-gather.15.cloned.1.call-update) | async-done | bytes 1048592 | tf_op jit(solution)/shard_map/all_gather | solution.py:34
  102.8 1.3 reshape.54
  104.1 137.8 %all-gather.11.cloned.1.call-done = bf16[1,4096,512]{2,1,0:T(8,128)(2,1)} async-done(((bf16[1,256,512]{2,1,0:T(8,128)(2,1)}), bf16[1,4096,512]{2,1,0:T(8,128)(2,1)}) %all-gather.11.cloned.1.call-update) | async-done | bytes 4194320 | tf_op jit(solution)/shard_map/all_gather | solution.py:30
  241.9 0.0 copy-done.1
  241.9 0.0 copy-done.2
  241.9 2.9 fusion.17
  244.9 0.1 copy.43
  245.0 129.6 %all-gather.9.cloned.1.call-done = bf16[1,4096,512]{2,1,0:T(8,128)(2,1)} async-done(((bf16[1,256,512]{2,1,0:T(8,128)(2,1)}), bf16[1,4096,512]{2,1,0:T(8,128)(2,1)}) %all-gather.9.cloned.1.call-update) | async-done | bytes 4194320 | tf_op jit(solution)/shard_map/all_gather | solution.py:31
  374.6 2.9 fusion.14
  377.5 0.1 copy.42
  377.6 0.2 fusion.27
  377.9 0.1 fusion.46
  378.0 129.1 %all-gather.13.cloned.1.call-done = bf16[1,4096,512]{2,1,0:T(8,128)(2,1)} async-done(((bf16[1,256,512]{2,1,0:T(8,128)(2,1)}), bf16[1,4096,512]{2,1,0:T(8,128)(2,1)}) %all-gather.13.cloned.1.call-update) | async-done | bytes 4194320 | tf_op jit(solution)/shard_map/all_gather | solution.py:32
  507.1 2.9 fusion.20
  510.0 0.2 convolution_bitcast_fusion
  510.2 0.2 convolution_convert_fusion.3
  510.4 4.7 convolution_convert_fusion
  515.1 0.0 all-reduce.4.cloned.1.call-update
  515.1 0.0 all-reduce.6.cloned.1.call-start
  515.2 0.2 fusion.23
  515.4 0.1 copy.39
  515.5 0.2 convolution_convert_fusion.2
  515.7 0.0 copy-start
  515.8 3.8 fusion.8
  519.6 0.0 copy-done
  519.6 2.5 fusion.1
  522.1 0.0 all-reduce.6.cloned.1.call-update
  522.1 1.3 dynamic-slice
  524.0 61.0 %all-reduce.4.cloned.1.call-done = bf16[128,4096]{1,0:T(8,128)(2,1)} async-done(((bf16[128,4096]{1,0:T(8,128)(2,1)}), bf16[128,4096]{1,0:T(8,128)(2,1)}) %all-reduce.4.cloned.1.call-update) | async-done | bytes 1048592 | tf_op jit(solution)/shard_map/psum | solution.py:79
  585.0 3.1 fusion.12
  588.1 53.1 %psum.15 = f32[1,1024]{1,0:T(1,128)} all-reduce(f32[1,1024]{1,0:T(1,128)S(1)} %bitcast.79), channel_id=1, replica_groups=mesh['dp'=16,'pipe'=8,'tensor'=4] {'dp'}, use_global_device_ids=true, to_apply=%region_7.0 | all-reduce | flops 1024 | bytes 8192 | tf_op jit(solution)/shard_map/psum | solution.py:87
  641.1 2.0 fusion.35
  643.1 227.7 %all-reduce.6.cloned.1.call-done = bf16[128,4096]{1,0:T(8,128)(2,1)} async-done(((bf16[128,4096]{1,0:T(8,128)(2,1)}), bf16[128,4096]{1,0:T(8,128)(2,1)}) %all-reduce.6.cloned.1.call-update) | async-done | bytes 1048592
  870.8 1.5 dynamic-slice_convert_fusion
  (3 shorter events, 0.0 us)
Async XLA Ops:
  7.2 95.6 %all-gather.15.cloned.1.call-start = ((), (), s32[]{:S(2)}) async-start(), calls=%async_computation.4 | async-start | bytes 1081344 | tf_op jit(solution)/shard_map/all_gather | solution.py:34
  7.9 234.0 %copy-start.1 = (bf16[1,128,4096]{2,1,0:T(8,128)(2,1)S(1)}, bf16[1,128,4096]{2,1,0:T(8,128)(2,1)}, u32[]{:S(2)}) copy-start(bf16[1,128,4096]{2,1,0:T(8,128)(2,1)} %param.8) | copy-start | bytes 3145732
  7.9 234.0 %copy-start.2 = (f32[1,4096]{1,0:T(1,128)S(1)}, f32[1,4096]{1,0:T(1,128)}, u32[]{:S(2)}) copy-start(f32[1,4096]{1,0:T(1,128)} %param.12) | copy-start | bytes 49156
  7.9 234.0 %all-gather.11.cloned.1.call-start = ((), (), s32[]{:S(2)}) async-start(), calls=%async_computation.2 | async-start | bytes 4456448 | tf_op jit(solution)/shard_map/all_gather | solution.py:30
  8.7 365.9 %all-gather.9.cloned.1.call-start = ((), (), s32[]{:S(2)}) async-start(), calls=%async_computation.1 | async-start | bytes 4456448 | tf_op jit(solution)/shard_map/all_gather | solution.py:31
  9.4 497.7 %all-gather.13.cloned.1.call-start = ((), (), s32[]{:S(2)}) async-start(), calls=%async_computation.3 | async-start | bytes 4456448 | tf_op jit(solution)/shard_map/all_gather | solution.py:32
  10.0 575.0 %all-reduce.4.cloned.1.call-start = ((), (), s32[]{:S(2)}) async-start(), calls=%async_computation | async-start | bytes 2097152 | tf_op jit(solution)/shard_map/psum | solution.py:79
  515.1 355.7 %all-reduce.6.cloned.1.call-start = ((), (), s32[]{:S(2)}) async-start(), calls=%async_computation.5 | async-start | bytes 2097152
  515.7 3.8 copy-start
Sparse Core Ops, SparseCore 0:
  10.1 92.6 all-gather.14
  105.8 136.1 all-gather.10
  245.0 129.5 all-gather.8
  377.4 129.5 all-gather.12
  515.3 69.7 all-reduce.3
  588.0 282.7 all-reduce.5
where the time goes:
time: 888 us; the launch traced here: 879 us
  waiting for transfers between devices  778 us (88%)
  blocking collectives  53.1 us (6%)
  matrix products  20.8 us (2%)
  between operations  14.9 us (2%)
    unnamed x7, waiting for transfers between devices  230 us
    all_gather x1, waiting for transfers between devices, shards(): lax.all_gather(query_weight[0], 'dp', axis=0, tiled=True)  138 us
    all_gather x1, waiting for transfers between devices, shards(): lax.all_gather(key_weight[0], 'dp', axis=0, tiled=True)  130 us
    all_gather x1, waiting for transfers between devices, shards(): lax.all_gather(value_weight[0], 'dp', axis=0, tiled=True)  129 us
    all_gather x1, waiting for transfers between devices, shards(): enc_full = lax.all_gather(encoder, ('pipe', 'tensor'), axis=0, tiled=True)  90.3 us
    psum x1, waiting for transfers between devices, shards(): lax.psum(hidden_part.astype(jnp.bfloat16), 'tensor').astype(jnp.float32)  61 us
    psum x1, blocking collectives, shards(): gain_total = lax.psum(gain_part, 'dp')  53.1 us
  transfers between devices with their start and end apart: 6, of which 6 were waited for; matrix products, arithmetic and copies ran while one was open for 3% of the time, Pallas kernels for 0%

commit v1 on v0

v1 whole, which is shorter than its diff:
```python
import functools
import math

import jax
import jax.numpy as jnp
from jax import lax
from jax.experimental import pallas as pl
from jax.experimental.pallas import tpu as pltpu
from jax.sharding import PartitionSpec as P

HEAD_DIM = 256
HEADS_HERE = 2
COLS = 512
D = 4096
ROWS = 128
SHARD = 256
BLOCK = 1024
EPSILON = 1e-06

SUBS = 4
CHUNK = SHARD // SUBS
HALF = CHUNK // 2
CHUNKS = 3 * SUBS
Z_AHEAD = 2
X_AHEAD = 4
MESH = pl.DeviceIdType.MESH


def dot_nt(left, right):
    return lax.dot_general(
        left, right, (((1,), (1,)), ((), ())), preferred_element_type=jnp.float32
    )


def dot_tn(left, right):
    return lax.dot_general(
        left, right, (((0,), (0,)), ((), ())), preferred_element_type=jnp.float32
    )


def regroup(rows):
    i = lax.broadcasted_iota(jnp.int32, (64, 64), 0)
    j = lax.broadcasted_iota(jnp.int32, (64, 64), 1)
    source = (i % 16) // 4 * 16 + i // 16 * 4 + i % 4
    hot = jnp.where(j == source, 1.0, 0.0).astype(jnp.bfloat16)
    return jnp.dot(hot, rows, preferred_element_type=jnp.float32)


def kernel(
    x_hbm, og_hbm, hg_hbm, enc_hbm, gain_ref, wq_hbm, wk_hbm, wv_hbm,
    ig_ref, eg_ref, gg_ref,
    w, xv, og, hg, enc64, enc, hid, inv, acc, qb, kb, vb, dq, dk, dv,
    hp, hp_in, inner, de, de1, de1_in, de2, de2_in, de3, de3_in, gz, gx,
    local, z_send, x_send, z_near, z_far, x_near, x_far,
    e_send, e_recv, h_send, h_recv, i_send, i_recv, d_send, d_recv, g_send, g_recv,
):
    dp = lax.axis_index("dp")
    pipe = lax.axis_index("pipe")
    t = lax.axis_index("tensor")
    x, z = dp // 4, dp % 4
    y, core = pipe // 2, pipe % 2

    def at_z(k):
        return (x * 4 + (z + k) % 4, pipe, t)

    def at_x(k):
        return ((x + k) % 4 * 4 + z, pipe, t)

    def at_y(k):
        return (dp, (y + k) % 4 * 2 + core, t)

    def at_t(k):
        return (dp, pipe, (t + k) % 4)

    other_core = (dp, y * 2 + 1 - core, t)

    loads = [
        pltpu.make_async_copy(
            ref.at[0], w.at[m, pl.ds(pl.multiple_of(dp * SHARD, SHARD), SHARD)], local.at[m]
        )
        for m, ref in enumerate((wq_hbm, wk_hbm, wv_hbm))
    ]
    enc_own = pltpu.make_async_copy(
        enc_hbm, enc64.at[pl.ds(pl.multiple_of(t * 16, 16), 16)], local.at[3]
    )
    x_load = pltpu.make_async_copy(x_hbm.at[0], xv, local.at[4])
    hg_load = pltpu.make_async_copy(hg_hbm.at[0], hg, local.at[5])
    og_load = pltpu.make_async_copy(
        og_hbm.at[0, :, pl.ds(pl.multiple_of(t * BLOCK, BLOCK), BLOCK)], og, local.at[6]
    )
    for copy in loads + [enc_own, x_load, hg_load, og_load]:
        copy.start()

    barrier = pltpu.get_barrier_semaphore()
    for k in range(1, 4):
        for peer in (at_z(k), at_x(k), at_y(k), at_t(k)):
            pl.semaphore_signal(barrier, inc=1, device_id=peer, device_id_type=MESH)
    pl.semaphore_signal(barrier, inc=1, device_id=other_core, device_id_type=MESH)
    for copy in loads + [enc_own]:
        copy.wait()
    pl.semaphore_wait(barrier, 13)

    def remote(src, dst, send, recv, peer):
        return pltpu.make_async_remote_copy(
            src_ref=src, dst_ref=dst, send_sem=send, recv_sem=recv,
            device_id=peer, device_id_type=MESH,
        )

    def piece(c, xx, zz, start=0, rows=CHUNK):
        first = (xx * 4 + zz) * SHARD + (c % SUBS) * CHUNK + start
        return w.at[c // SUBS, pl.ds(pl.multiple_of(first, HALF), rows)]

    def wait_bytes(sem, rows):
        part = w.at[0, pl.ds(0, rows)]
        pltpu.make_async_copy(part, part, sem).wait()

    def z_first(c):
        own = piece(c, x, z)
        for k in (1, -1):
            remote(own, own, z_send.at[c], z_near.at[c], at_z(k)).start()

    def z_second(c):
        up = piece(c, x, (z + 3) % 4, HALF, HALF)
        remote(up, up, z_send.at[c], z_far.at[c], at_z(1)).start()
        down = piece(c, x, (z + 1) % 4, 0, HALF)
        remote(down, down, z_send.at[c], z_far.at[c], at_z(-1)).start()

    def x_first(c, j):
        own = piece(c, x, (z + j) % 4)
        for k in (1, -1):
            remote(own, own, x_send.at[c], x_near.at[j, c], at_x(k)).start()

    def x_second(c, j):
        up = piece(c, (x + 3) % 4, (z + j) % 4, HALF, HALF)
        remote(up, up, x_send.at[c], x_far.at[j, c], at_x(1)).start()
        down = piece(c, (x + 1) % 4, (z + j) % 4, 0, HALF)
        remote(down, down, x_send.at[c], x_far.at[j, c], at_x(-1)).start()

    for c in range(Z_AHEAD):
        z_first(c)
    for c in range(X_AHEAD):
        x_first(c, 0)

    def enc_rows(p):
        return enc.at[pl.ds(pl.multiple_of(p * 16, 16), 16)]

    own16 = enc64.at[pl.ds(pl.multiple_of(t * 16, 16), 16)]
    for k in range(1, 4):
        remote(own16, own16, e_send.at[0], e_recv.at[0], at_t(k)).start()

    def enc_y():
        rows48 = enc64.at[pl.ds(0, 48)]
        pltpu.make_async_copy(rows48, rows48, e_recv.at[0]).wait()
        moved = regroup(enc64[...]).astype(jnp.bfloat16)
        for b in range(4):
            enc[pl.ds(pl.multiple_of(pipe * 16, 16), 16), b * BLOCK : (b + 1) * BLOCK] = moved[
                b * 16 : (b + 1) * 16
            ]
        mine = enc_rows(pipe)
        for k in range(1, 4):
            remote(mine, mine, e_send.at[1], e_recv.at[1], at_y(k)).start()

    def enc_core():
        rows48 = enc.at[pl.ds(0, 48)]
        pltpu.make_async_copy(rows48, rows48, e_recv.at[1]).wait()
        for k in range(4):
            mine = enc_rows(k * 2 + core)
            remote(mine, mine, e_send.at[2], e_recv.at[2], other_core).start()

    def enc_wait():
        rows64 = enc.at[pl.ds(0, 64)]
        pltpu.make_async_copy(rows64, rows64, e_recv.at[2]).wait()

    def norm():
        x_load.wait()
        total = jnp.zeros((ROWS, 1), jnp.float32)
        for b in range(4):
            part = xv[:, b * BLOCK : (b + 1) * BLOCK].astype(jnp.float32)
            total += jnp.sum(part * part, axis=1, keepdims=True)
        scale = lax.rsqrt(total / D + EPSILON)
        inv[...] = jnp.broadcast_to(scale, (ROWS, 128))
        for b in range(4):
            cols = slice(b * BLOCK, (b + 1) * BLOCK)
            normed = xv[:, cols].astype(jnp.float32) * scale
            hid[:, cols] = (normed * gain_ref[:, cols]).astype(jnp.bfloat16)

    def project(left, m, out):
        acc[...] = jnp.zeros_like(acc)

        @pl.loop(0, D // COLS)
        def _(k):
            at = pl.ds(pl.multiple_of(k * COLS, COLS), COLS)
            acc[...] += jnp.dot(left[:, at], w[m, at, :], preferred_element_type=jnp.float32)

        out[...] = acc[...].astype(jnp.bfloat16)

    steps = CHUNKS + 3

    @pl.loop(0, steps)
    def _(c):
        @pl.when(c < CHUNKS)
        def _():
            wait_bytes(z_near.at[c], 2 * CHUNK)
            z_second(c)

            @pl.when(c + Z_AHEAD < CHUNKS)
            def _():
                z_first(c + Z_AHEAD)

            x_first(c, 1)
            x_first(c, 3)
            wait_bytes(x_near.at[0, c], 2 * CHUNK)
            x_second(c, 0)

            @pl.when(c + X_AHEAD < CHUNKS)
            def _():
                x_first(c + X_AHEAD, 0)

        @pl.when(jnp.logical_and(c >= 1, c < CHUNKS + 1))
        def _():
            b = c - 1
            wait_bytes(z_far.at[b], CHUNK)
            x_first(b, 2)
            for j in (1, 3):
                wait_bytes(x_near.at[j, b], 2 * CHUNK)
                x_second(b, j)

        @pl.when(jnp.logical_and(c >= 2, c < CHUNKS + 2))
        def _():
            b = c - 2
            wait_bytes(x_near.at[2, b], 2 * CHUNK)
            x_second(b, 2)

        @pl.when(c >= 3)
        def _():
            b = c - 3
            for j in range(4):
                wait_bytes(x_far.at[j, b], CHUNK)

        pl.when(c == 0)(enc_y)
        pl.when(c == 1)(enc_core)
        pl.when(c == 2)(norm)

        @pl.when(c == SUBS + 2)
        def _():
            enc_wait()
            project(hid, 0, qb)

        @pl.when(c == 2 * SUBS + 2)
        def _():
            project(enc, 1, kb)

    project(enc, 2, vb)
    hg_load.wait()

    scale = 1.0 / math.sqrt(HEAD_DIM)
    for h in range(HEADS_HERE):
        cols = slice(h * HEAD_DIM, (h + 1) * HEAD_DIM)
        q, k, v, a = qb[:, cols], kb[:, cols], vb[:, cols], hg[:, cols]
        expo = jnp.exp(dot_nt(q, k) * scale)
        probs = expo / jnp.sum(expo, axis=1, keepdims=True)
        prob_grad = dot_nt(a, v)
        mean = jnp.sum(prob_grad * probs, axis=1, keepdims=True)
        score_grad = (probs * (prob_grad - mean) * scale).astype(jnp.bfloat16)
        dq[:, cols] = jnp.dot(score_grad, k, preferred_element_type=jnp.float32).astype(jnp.bfloat16)
        dk[:, cols] = dot_tn(score_grad, q).astype(jnp.bfloat16)
        dv[:, cols] = dot_tn(probs.astype(jnp.bfloat16), a).astype(jnp.bfloat16)

    inner[0] = jnp.zeros((ROWS, 128), jnp.float32)

    def hidden_block(j):
        at = pl.ds(pl.multiple_of(j * BLOCK, BLOCK), BLOCK)
        part = dot_nt(dq[...], w[0, at, :]).astype(jnp.bfloat16)
        hp[j] = part
        normed = xv[:, at].astype(jnp.float32) * inv[:, :1]
        product = part.astype(jnp.float32) * gain_ref[:, at] * normed
        folded = product[:, :128]
        for b in range(1, BLOCK // 128):
            folded += product[:, b * 128 : (b + 1) * 128]
        inner[0] += folded

    @pl.loop(1, 4)
    def _(k):
        j = (t + k) % 4
        hidden_block(j)
        remote(hp.at[j], hp_in.at[t], h_send.at[0], h_recv.at[0], at_t(k)).start()

    hidden_block(t)
    row = jnp.sum(inner[0].T, axis=0, keepdims=True)
    inner[1, pl.ds(0, 8)] = jnp.broadcast_to(row, (8, 128))
    for k in range(1, 4):
        remote(
            inner.at[1, pl.ds(0, 8)], inner.at[2, pl.ds(pl.multiple_of(t * 8, 8), 8)],
            i_send.at[0], i_recv.at[0], at_t(k),
        ).start()

    @pl.loop(0, D // COLS)
    def _(b):
        at = pl.ds(pl.multiple_of(b * COLS, COLS), COLS)
        de[:, at] = dot_nt(dk[...], w[1, at, :]) + dot_nt(dv[...], w[2, at, :])

    def pair_rows(k, c):
        return pl.ds(pl.multiple_of((k * 2 + c) * 16, 16), 16)

    for k in range(4):
        de1[k] = de[pair_rows(k, 1 - core), :].astype(jnp.bfloat16)
    remote(de1, de1_in, d_send.at[0], d_recv.at[0], other_core).start()
    pltpu.make_async_copy(de1_in, de1_in, d_recv.at[0]).wait()

    for k in range(1, 4):
        to = (y + k) % 4
        de2[to] = (de[pair_rows(to, core), :] + de1_in[to].astype(jnp.float32)).astype(jnp.bfloat16)
        remote(de2.at[to], de2_in.at[y], d_send.at[1], d_recv.at[1], at_y(k)).start()
    total = de[pair_rows(y, core), :] + de1_in[y].astype(jnp.float32)
    three = de2_in.at[pl.ds(0, 3)]
    pltpu.make_async_copy(three, three, d_recv.at[1]).wait()
    for k in range(1, 4):
        total += de2_in[(y + k) % 4].astype(jnp.float32)
    low = total.astype(jnp.bfloat16)
    stacked = jnp.concatenate([low[:, b * BLOCK : (b + 1) * BLOCK] for b in range(4)], axis=0)
    moved = regroup(stacked).astype(jnp.bfloat16)
    for b in range(4):
        de3[b] = moved[b * 16 : (b + 1) * 16]
    for k in range(1, 4):
        remote(
            de3.at[(t + k) % 4], de3_in.at[t], d_send.at[2], d_recv.at[2], at_t(k)
        ).start()

    og_load.wait()
    rows24 = inner.at[2, pl.ds(0, 24)]
    pltpu.make_async_copy(rows24, rows24, i_recv.at[0]).wait()
    row_total = row
    for k in range(1, 4):
        row_total += inner[2, pl.ds(pl.multiple_of((t + k) % 4 * 8, 8), 1)]
    mean = jnp.broadcast_to(row_total / D, (128, 128)).T[:, :1]
    three = hp_in.at[pl.ds(0, 3)]
    pltpu.make_async_copy(three, three, h_recv.at[0]).wait()
    hidden_grad = hp[t].astype(jnp.float32)
    for k in range(1, 4):
        hidden_grad += hp_in[(t + k) % 4].astype(jnp.float32)
    at = pl.ds(pl.multiple_of(t * BLOCK, BLOCK), BLOCK)
    scale_col = inv[:, :1]
    normed = xv[:, at].astype(jnp.float32) * scale_col
    own_gain = jnp.sum(hidden_grad * normed, axis=0, keepdims=True)
    gz[z] = own_gain
    for k in range(1, 4):
        remote(gz.at[z], gz.at[z], g_send.at[0], g_recv.at[0], at_z(k)).start()
    normed_grad = hidden_grad * gain_ref[:, at]
    ig_ref[0] = (
        og[...].astype(jnp.float32) + scale_col * (normed_grad - normed * mean)
    ).astype(jnp.bfloat16)

    three = gz.at[pl.ds(0, 3)]
    pltpu.make_async_copy(three, three, g_recv.at[0]).wait()
    gx[x] = gz[0] + gz[1] + gz[2] + gz[3]
    for k in range(1, 4):
        remote(gx.at[x], gx.at[x], g_send.at[1], g_recv.at[1], at_x(k)).start()

    three = de3_in.at[pl.ds(0, 3)]
    pltpu.make_async_copy(three, three, d_recv.at[2]).wait()
    summed = de3[t].astype(jnp.float32)
    for k in range(1, 4):
        summed += de3_in[(t + k) % 4].astype(jnp.float32)
    eg_ref[...] = summed

    three = gx.at[pl.ds(0, 3)]
    pltpu.make_async_copy(three, three, g_recv.at[1]).wait()
    gg_ref[...] = gx[0] + gx[1] + gx[2] + gx[3]

    @pl.loop(0, CHUNKS)
    def _(c):
        wait_bytes(z_send.at[c], 3 * CHUNK)
        wait_bytes(x_send.at[c], 12 * CHUNK)

    def sent(ref, sem):
        pltpu.make_async_copy(ref, ref, sem).wait()

    sent(enc64.at[pl.ds(0, 48)], e_send.at[0])
    sent(enc.at[pl.ds(0, 48)], e_send.at[1])
    sent(enc.at[pl.ds(0, 64)], e_send.at[2])
    sent(hp.at[pl.ds(0, 3)], h_send.at[0])
    sent(inner.at[2, pl.ds(0, 24)], i_send.at[0])
    sent(de1, d_send.at[0])
    sent(de2.at[pl.ds(0, 3)], d_send.at[1])
    sent(de3.at[pl.ds(0, 3)], d_send.at[2])
    sent(gz.at[pl.ds(0, 3)], g_send.at[0])
    sent(gx.at[pl.ds(0, 3)], g_send.at[1])


def shards(
    section_input, out_grad, head_grad, encoder, norm_gain, query_weight, key_weight, value_weight
):
    low, f32 = jnp.bfloat16, jnp.float32
    enc16 = encoder.reshape(4, 4, BLOCK).transpose(1, 0, 2).reshape(16, BLOCK)
    hbm = pl.BlockSpec(memory_space=pl.ANY)
    vmem = pl.BlockSpec(memory_space=pltpu.VMEM)
    dma = pltpu.SemaphoreType.DMA
    grads = pl.pallas_call(
        kernel,
        out_shape=(
            jax.ShapeDtypeStruct((1, ROWS, BLOCK), low),
            jax.ShapeDtypeStruct((16, BLOCK), f32),
            jax.ShapeDtypeStruct((1, BLOCK), f32),
        ),
        in_specs=[hbm, hbm, hbm, hbm, vmem, hbm, hbm, hbm],
        out_specs=(vmem, vmem, vmem),
        scratch_shapes=[
            pltpu.VMEM((3, D, COLS), low),
            pltpu.VMEM((ROWS, D), low),
            pltpu.VMEM((ROWS, BLOCK), low),
            pltpu.VMEM((ROWS, COLS), low),
            pltpu.VMEM((64, BLOCK), low),
            pltpu.VMEM((ROWS, D), low),
            pltpu.VMEM((ROWS, D), low),
            pltpu.VMEM((ROWS, 128), f32),
            pltpu.VMEM((ROWS, COLS), f32),
        ]
        + [pltpu.VMEM((ROWS, COLS), low)] * 6
        + [
            pltpu.VMEM((4, ROWS, BLOCK), low),
            pltpu.VMEM((4, ROWS, BLOCK), low),
            pltpu.VMEM((3, ROWS, 128), f32),
            pltpu.VMEM((ROWS, D), f32),
            pltpu.VMEM((4, 16, D), low),
            pltpu.VMEM((4, 16, D), low),
            pltpu.VMEM((4, 16, D), low),
            pltpu.VMEM((4, 16, D), low),
            pltpu.VMEM((4, 16, BLOCK), low),
            pltpu.VMEM((4, 16, BLOCK), low),
            pltpu.VMEM((4, 1, BLOCK), f32),
            pltpu.VMEM((4, 1, BLOCK), f32),
            dma((7,)),
            dma((CHUNKS,)),
            dma((CHUNKS,)),
            dma((CHUNKS,)),
            dma((CHUNKS,)),
            dma((4, CHUNKS)),
            dma((4, CHUNKS)),
            dma((3,)),
            dma((3,)),
            dma((1,)),
            dma((1,)),
            dma((1,)),
            dma((1,)),
            dma((3,)),
            dma((3,)),
            dma((2,)),
            dma((2,)),
        ],
        compiler_params=pltpu.CompilerParams(
            collective_id=0, has_side_effects=True, vmem_limit_bytes=48 * 1024 * 1024
        ),
        cost_estimate=pl.CostEstimate(
            flops=6 * 2 * ROWS * D * COLS, bytes_accessed=4 * 1024 * 1024, transcendentals=0
        ),
    )(
        section_input, out_grad, head_grad, enc16, norm_gain,
        query_weight, key_weight, value_weight,
    )
    input_grad, enc_grad, gain_grad = grads
    enc_grad = enc_grad.reshape(4, 4, BLOCK).transpose(1, 0, 2).reshape(4, D)
    return input_grad, enc_grad, gain_grad


def solution(mesh):
    placed = (
        P("pipe", "dp", None),
        P("pipe", "dp", None),
        P("pipe", "dp", "tensor"),
        P(("dp", "pipe", "tensor"), None),
        P("pipe", None),
        P("pipe", "dp", "tensor"),
        P("pipe", "dp", "tensor"),
        P("pipe", "dp", "tensor"),
    )
    return jax.shard_map(
        shards,
        mesh=mesh,
        in_specs=placed,
        out_specs=(
            P("pipe", "dp", "tensor"),
            P(("dp", "pipe", "tensor"), None),
            P("pipe", "tensor"),
        ),
        check_vma=False,
    )
```

time: 888 us -> 192 us (0.22)
  the two profiles are of different devices: /device:TPU:24 before, /device:TPU:4 now
where the time goes in v1:
time: 192 us; the launch traced here: 191 us
  Pallas kernels  182 us (95%)
  local copies, waits for them, and re-layouts  8.92 us (5%)
    pallas_call x1, Pallas kernels, shards(): pl.pallas_call(kernel, out_shape=(jax.ShapeDtypeStruct((1, ROWS, BLOCK),...  182 us
    unnamed x16, local copies, waits for them, and re-layouts  7.49 us

profile of v1, /device:TPU:4, one launch (start us, length us, event | category | flops | bytes accessed | tf_op | source)
XLA Modules:
  0.0 191.4 jit_solution(4521665646408234823)
XLA Ops:
  0.6 0.0 copy-start.6
  0.6 0.8 reshape.19.enc_hbm
  1.4 0.0 copy-done.6
  1.4 0.0 copy-start
  1.4 1.2 copy-done
  2.7 0.0 copy-start.1
  2.7 1.2 copy-done.1
  3.9 0.0 copy-start.2
  3.9 0.9 copy-done.2
  4.8 0.0 copy-start.3
  4.8 0.9 copy-done.3
  5.8 0.0 copy-start.4
  5.8 0.9 copy-done.4
  6.7 0.0 copy-start.5
  6.7 0.9 copy-done.5
  7.6 181.8 %shard_map.103 = (bf16[1,128,1024]{2,1,0:T(8,128)(2,1)S(1)}, f32[16,1024]{1,0:T(8,128)S(1)}, f32[1,1024]{1,0:T(1,128)S(1)}) custom-call(bf16[1,128,4096]{2,1,0:T(8,128)(2,1)S(1)} %copy-done, bf16[1,128,4096]{2,1,0:T(8,128)(2,1)S(1)} %copy-done.1, bf16[1,128,512]{2,1,0:T(8,128)(2,1)S(1)} %copy-done.5, bf16[16,1024]{1,0:T(8,128)(2,1)S(1)} %reshape.19.enc_hbm, ...), custom_call_target="tpu_custom_call" | custom-call | flops 3221225472 | bytes 4194304 | tf_op jit(solution)/shard_map/pallas_call | solution.py:398
  189.5 0.7 reshape.20
  190.1 0.7 copy.15
  190.8 0.6 copy.16
Async XLA Ops:
  0.6 0.8 copy-start.6
  1.4 1.2 copy-start
  2.7 1.2 copy-start.1
  3.9 0.9 copy-start.2
  4.8 0.9 copy-start.3
  5.8 0.9 copy-start.4
  6.7 0.9 copy-start.5

commit v2 on v1

--- a/solution.py
+++ b/solution.py
@@ -22,7 +22,7 @@
 HALF = CHUNK // 2
 CHUNKS = 3 * SUBS
 Z_AHEAD = 2
-X_AHEAD = 4
+X_AHEAD = 12
 MESH = pl.DeviceIdType.MESH
 
 
@@ -50,7 +50,7 @@
     x_hbm, og_hbm, hg_hbm, enc_hbm, gain_ref, wq_hbm, wk_hbm, wv_hbm,
     ig_ref, eg_ref, gg_ref,
     w, xv, og, hg, enc64, enc, hid, inv, acc, qb, kb, vb, dq, dk, dv,
-    hp, hp_in, inner, de, de1, de1_in, de2, de2_in, de3, de3_in, gz, gx,
+    hp, hp_in, note, note_in, de, de1, de1_in, de2, de2_in, de3, de3_in, gz, gx,
     local, z_send, x_send, z_near, z_far, x_near, x_far,
     e_send, e_recv, h_send, h_recv, i_send, i_recv, d_send, d_recv, g_send, g_recv,
 ):
@@ -266,32 +266,36 @@
         dk[:, cols] = dot_tn(score_grad, q).astype(jnp.bfloat16)
         dv[:, cols] = dot_tn(probs.astype(jnp.bfloat16), a).astype(jnp.bfloat16)
 
-    inner[0] = jnp.zeros((ROWS, 128), jnp.float32)
+    note[...] = jnp.zeros_like(note)
 
     def hidden_block(j):
         at = pl.ds(pl.multiple_of(j * BLOCK, BLOCK), BLOCK)
         part = dot_nt(dq[...], w[0, at, :]).astype(jnp.bfloat16)
         hp[j] = part
-        normed = xv[:, at].astype(jnp.float32) * inv[:, :1]
-        product = part.astype(jnp.float32) * gain_ref[:, at] * normed
+        product = part.astype(jnp.float32) * (xv[:, at].astype(jnp.float32) * inv[:, :1])
+        gain = jnp.sum(product, axis=0, keepdims=True)
+        product *= gain_ref[:, at]
         folded = product[:, :128]
-        for b in range(1, BLOCK // 128):
-            folded += product[:, b * 128 : (b + 1) * 128]
-        inner[0] += folded
-
-    @pl.loop(1, 4)
-    def _(k):
+        for b in range(8):
+            note[j, pl.ds(8 + b, 1)] = gain[:, b * 128 : (b + 1) * 128]
+            if b:
+                folded += product[:, b * 128 : (b + 1) * 128]
+        return folded
+
+    def hidden_step(k, folded):
         j = (t + k) % 4
-        hidden_block(j)
+        folded += hidden_block(j)
         remote(hp.at[j], hp_in.at[t], h_send.at[0], h_recv.at[0], at_t(k)).start()
-
-    hidden_block(t)
-    row = jnp.sum(inner[0].T, axis=0, keepdims=True)
-    inner[1, pl.ds(0, 8)] = jnp.broadcast_to(row, (8, 128))
+        return folded
+
+    folded = lax.fori_loop(1, 4, hidden_step, jnp.zeros((ROWS, 128), jnp.float32))
+    folded += hidden_block(t)
+    row = jnp.sum(folded.T, axis=0, keepdims=True)
+    for j in range(4):
+        note[j, pl.ds(0, 1)] = row
     for k in range(1, 4):
         remote(
-            inner.at[1, pl.ds(0, 8)], inner.at[2, pl.ds(pl.multiple_of(t * 8, 8), 8)],
-            i_send.at[0], i_recv.at[0], at_t(k),
+            note.at[(t + k) % 4], note_in.at[t], i_send.at[0], i_recv.at[0], at_t(k)
         ).start()
 
     @pl.loop(0, D // COLS)
@@ -302,18 +306,35 @@
     def pair_rows(k, c):
         return pl.ds(pl.multiple_of((k * 2 + c) * 16, 16), 16)
 
+    def arrived(ref, sem):
+        three = ref.at[pl.ds(0, 3)]
+        pltpu.make_async_copy(three, three, sem).wait()
+
     for k in range(4):
         de1[k] = de[pair_rows(k, 1 - core), :].astype(jnp.bfloat16)
     remote(de1, de1_in, d_send.at[0], d_recv.at[0], other_core).start()
+
+    arrived(note_in, i_recv.at[0])
+    note_in[t] = note[t]
+    noted = note_in[0] + note_in[1] + note_in[2] + note_in[3]
+    gz[z] = noted[8:]
+    for k in range(1, 4):
+        remote(gz.at[z], gz.at[z], g_send.at[0], g_recv.at[0], at_z(k)).start()
+    mean = jnp.broadcast_to(noted[:1] / D, (128, 128)).T[:, :1]
+
     pltpu.make_async_copy(de1_in, de1_in, d_recv.at[0]).wait()
-
     for k in range(1, 4):
         to = (y + k) % 4
         de2[to] = (de[pair_rows(to, core), :] + de1_in[to].astype(jnp.float32)).astype(jnp.bfloat16)
         remote(de2.at[to], de2_in.at[y], d_send.at[1], d_recv.at[1], at_y(k)).start()
     total = de[pair_rows(y, core), :] + de1_in[y].astype(jnp.float32)
-    three = de2_in.at[pl.ds(0, 3)]
-    pltpu.make_async_copy(three, three, d_recv.at[1]).wait()
+
+    arrived(gz, g_recv.at[0])
+    gx[x] = gz[0] + gz[1] + gz[2] + gz[3]
+    for k in range(1, 4):
+        remote(gx.at[x], gx.at[x], g_send.at[1], g_recv.at[1], at_x(k)).start()
+
+    arrived(de2_in, d_recv.at[1])
     for k in range(1, 4):
         total += de2_in[(y + k) % 4].astype(jnp.float32)
     low = total.astype(jnp.bfloat16)
@@ -325,47 +346,29 @@
         remote(
             de3.at[(t + k) % 4], de3_in.at[t], d_send.at[2], d_recv.at[2], at_t(k)
         ).start()
+    arrived(gx, g_recv.at[1])
+    gains = gx[0] + gx[1] + gx[2] + gx[3]
+    for b in range(8):
+        gg_ref[:, b * 128 : (b + 1) * 128] = gains[b : b + 1]
 
     og_load.wait()
-    rows24 = inner.at[2, pl.ds(0, 24)]
-    pltpu.make_async_copy(rows24, rows24, i_recv.at[0]).wait()
-    row_total = row
-    for k in range(1, 4):
-        row_total += inner[2, pl.ds(pl.multiple_of((t + k) % 4 * 8, 8), 1)]
-    mean = jnp.broadcast_to(row_total / D, (128, 128)).T[:, :1]
-    three = hp_in.at[pl.ds(0, 3)]
-    pltpu.make_async_copy(three, three, h_recv.at[0]).wait()
-    hidden_grad = hp[t].astype(jnp.float32)
-    for k in range(1, 4):
-        hidden_grad += hp_in[(t + k) % 4].astype(jnp.float32)
     at = pl.ds(pl.multiple_of(t * BLOCK, BLOCK), BLOCK)
     scale_col = inv[:, :1]
     normed = xv[:, at].astype(jnp.float32) * scale_col
-    own_gain = jnp.sum(hidden_grad * normed, axis=0, keepdims=True)
-    gz[z] = own_gain
-    for k in range(1, 4):
-        remote(gz.at[z], gz.at[z], g_send.at[0], g_recv.at[0], at_z(k)).start()
+    arrived(hp_in, h_recv.at[0])
+    hidden_grad = hp[t].astype(jnp.float32)
+    for k in range(1, 4):
+        hidden_grad += hp_in[(t + k) % 4].astype(jnp.float32)
     normed_grad = hidden_grad * gain_ref[:, at]
     ig_ref[0] = (
         og[...].astype(jnp.float32) + scale_col * (normed_grad - normed * mean)
     ).astype(jnp.bfloat16)
 
-    three = gz.at[pl.ds(0, 3)]
-    pltpu.make_async_copy(three, three, g_recv.at[0]).wait()
-    gx[x] = gz[0] + gz[1] + gz[2] + gz[3]
-    for k in range(1, 4):
-        remote(gx.at[x], gx.at[x], g_send.at[1], g_recv.at[1], at_x(k)).start()
-
-    three = de3_in.at[pl.ds(0, 3)]
-    pltpu.make_async_copy(three, three, d_recv.at[2]).wait()
+    arrived(de3_in, d_recv.at[2])
     summed = de3[t].astype(jnp.float32)
     for k in range(1, 4):
         summed += de3_in[(t + k) % 4].astype(jnp.float32)
     eg_ref[...] = summed
-
-    three = gx.at[pl.ds(0, 3)]
-    pltpu.make_async_copy(three, three, g_recv.at[1]).wait()
-    gg_ref[...] = gx[0] + gx[1] + gx[2] + gx[3]
 
     @pl.loop(0, CHUNKS)
     def _(c):
@@ -379,7 +382,7 @@
     sent(enc.at[pl.ds(0, 48)], e_send.at[1])
     sent(enc.at[pl.ds(0, 64)], e_send.at[2])
     sent(hp.at[pl.ds(0, 3)], h_send.at[0])
-    sent(inner.at[2, pl.ds(0, 24)], i_send.at[0])
+    sent(note.at[pl.ds(0, 3)], i_send.at[0])
     sent(de1, d_send.at[0])
     sent(de2.at[pl.ds(0, 3)], d_send.at[1])
     sent(de3.at[pl.ds(0, 3)], d_send.at[2])
@@ -419,7 +422,8 @@
         + [
             pltpu.VMEM((4, ROWS, BLOCK), low),
             pltpu.VMEM((4, ROWS, BLOCK), low),
-            pltpu.VMEM((3, ROWS, 128), f32),
+            pltpu.VMEM((4, 16, 128), f32),
+            pltpu.VMEM((4, 16, 128), f32),
             pltpu.VMEM((ROWS, D), f32),
             pltpu.VMEM((4, 16, D), low),
             pltpu.VMEM((4, 16, D), low),
@@ -427,8 +431,8 @@
             pltpu.VMEM((4, 16, D), low),
             pltpu.VMEM((4, 16, BLOCK), low),
             pltpu.VMEM((4, 16, BLOCK), low),
-            pltpu.VMEM((4, 1, BLOCK), f32),
-            pltpu.VMEM((4, 1, BLOCK), f32),
+            pltpu.VMEM((4, 8, 128), f32),
+            pltpu.VMEM((4, 8, 128), f32),
             dma((7,)),
             dma((CHUNKS,)),
             dma((CHUNKS,)),
@@ -448,7 +452,7 @@
             dma((2,)),
         ],
         compiler_params=pltpu.CompilerParams(
-            collective_id=0, has_side_effects=True, vmem_limit_bytes=48 * 1024 * 1024
+            collective_id=0, has_side_effects=True, vmem_limit_bytes=60 * 1024 * 1024
         ),
         cost_estimate=pl.CostEstimate(
             flops=6 * 2 * ROWS * D * COLS, bytes_accessed=4 * 1024 * 1024, transcendentals=0

time: 192 us -> 183 us (0.953)
  the two profiles are of different devices: /device:TPU:4 before, /device:TPU:24 now
where the time goes in v2:
time: 183 us; the launch traced here: 180 us
  Pallas kernels  174 us (95%)
  local copies, waits for them, and re-layouts  5.14 us (3%)
    pallas_call x1, Pallas kernels, shards(): pl.pallas_call(kernel, out_shape=(jax.ShapeDtypeStruct((1, ROWS, BLOCK),...  174 us

profile of v2, /device:TPU:24, one launch (start us, length us, event | category | flops | bytes accessed | tf_op | source)
XLA Modules:
  0.0 180.2 jit_solution(14435738591372091972)
XLA Ops:
  0.6 1.4 reshape.19.enc_hbm
  2.0 174.4 %shard_map.103 = (bf16[1,128,1024]{2,1,0:T(8,128)(2,1)}, f32[16,1024]{1,0:T(8,128)}, f32[1,1024]{1,0:T(1,128)}) custom-call(bf16[1,128,4096]{2,1,0:T(8,128)(2,1)} %x_hbm.1, bf16[1,128,4096]{2,1,0:T(8,128)(2,1)} %og_hbm.1, bf16[1,128,512]{2,1,0:T(8,128)(2,1)} %hg_hbm.1, bf16[16,1024]{1,0:T(8,128)(2,1)} %reshape.19.enc_hbm, f32[1,4096]{1,0:T(1,128)} %gain_ref.1, ...), custom_call_target="tpu_custom_call" | custom-call | flops 3221225472 | bytes 4194304 | tf_op jit(solution)/shard_map/pallas_call | solution.py:401
  176.4 1.5 reshape.20
  177.9 0.0 copy-start
  177.9 1.7 copy.15
  179.6 0.0 copy-done
  179.6 0.6 copy.16
Async XLA Ops:
  177.9 1.7 copy-start

commit v3 on v2

v3 whole, which is shorter than its diff:
```python
import math

import jax
import jax.numpy as jnp
from jax import lax
from jax.experimental import pallas as pl
from jax.experimental.pallas import tpu as pltpu
from jax.sharding import PartitionSpec as P

HEAD_DIM = 256
HEADS_HERE = 2
COLS = 512
D = 4096
ROWS = 128
SHARD = 256
HALF = SHARD // 2
BLOCK = 1024
EPSILON = 1e-06
MESH = pl.DeviceIdType.MESH


def dot_nt(left, right):
    return lax.dot_general(
        left, right, (((1,), (1,)), ((), ())), preferred_element_type=jnp.float32
    )


def dot_tn(left, right):
    return lax.dot_general(
        left, right, (((0,), (0,)), ((), ())), preferred_element_type=jnp.float32
    )


def regroup(rows):
    i = lax.broadcasted_iota(jnp.int32, (64, 64), 0)
    j = lax.broadcasted_iota(jnp.int32, (64, 64), 1)
    source = (i % 16) // 4 * 16 + i // 16 * 4 + i % 4
    hot = jnp.where(j == source, 1.0, 0.0).astype(jnp.bfloat16)
    return jnp.dot(hot, rows, preferred_element_type=jnp.float32)


def kernel(
    x_hbm, og_hbm, hg_hbm, enc_ref, gain_ref, wq_hbm, wk_hbm, wv_hbm,
    ig_ref, eg_ref, gg_ref,
    wq, wkv, xv, og, hg, lines, enc64, encx, enc, hid, inv, part, part_in, kv, qb, probs, dq, dkv,
    hp, hp_in, note, note_in, de, de1, de1_in, de2, de2_in, dex, dex_in, de3, de3_in, gz, gx,
    local, z_send, x_send, z_near, z_far, x_near, x_far, p_send, p_recv, k_send, k_recv,
    e_send, e_recv, h_send, h_recv, i_send, i_recv, d_send, d_recv, g_send, g_recv,
):
    dp = lax.axis_index("dp")
    pipe = lax.axis_index("pipe")
    t = lax.axis_index("tensor")
    x, z = dp // 4, dp % 4
    y, core = pipe // 2, pipe % 2

    def at_z(k):
        return (x * 4 + (z + k) % 4, pipe, t)

    def at_x(k):
        return ((x + k) % 4 * 4 + z, pipe, t)

    def at_y(k):
        return (dp, (y + k) % 4 * 2 + core, t)

    def at_t(k):
        return (dp, pipe, (t + k) % 4)

    other_core = (dp, y * 2 + 1 - core, t)

    def remote(src, dst, send, recv, peer):
        return pltpu.make_async_remote_copy(
            src_ref=src, dst_ref=dst, send_sem=send, recv_sem=recv,
            device_id=peer, device_id_type=MESH,
        )

    def rows_of(ref, block, rows, start=0):
        return ref.at[pl.ds(pl.multiple_of(block * rows + start, 16), rows)]

    def wait_for(ref, sem):
        pltpu.make_async_copy(ref, ref, sem).wait()

    def arrived(ref, sem):
        wait_for(ref.at[pl.ds(0, 3)], sem)

    def piece(c, xx, zz, start=0, rows=SHARD):
        m, h = c // 2, c % 2
        if m == 0:
            first = (xx * 4 + zz) * SHARD + start
            return wq.at[h, pl.ds(pl.multiple_of(first, HALF), rows)]
        return wkv.at[m - 1, h, pl.ds(pl.multiple_of(zz * SHARD + start, HALF), rows)]

    sources = (wq_hbm, wk_hbm, wv_hbm)
    loads = [
        pltpu.make_async_copy(
            sources[c // 2].at[0, :, pl.ds(c % 2 * HEAD_DIM, HEAD_DIM)], piece(c, x, z), local.at[c]
        )
        for c in range(6)
    ]
    x_load = pltpu.make_async_copy(x_hbm.at[0], xv, local.at[7])
    hg_load = pltpu.make_async_copy(hg_hbm.at[0], hg, local.at[8])
    og_load = pltpu.make_async_copy(
        og_hbm.at[0, :, pl.ds(pl.multiple_of(t * BLOCK, BLOCK), BLOCK)], og, local.at[9]
    )
    for copy in loads + [x_load, hg_load, og_load]:
        copy.start()

    barrier = pltpu.get_barrier_semaphore()
    for k in range(1, 4):
        for peer in (at_z(k), at_x(k), at_y(k), at_t(k)):
            pl.semaphore_signal(barrier, inc=1, device_id=peer, device_id_type=MESH)
    pl.semaphore_signal(barrier, inc=1, device_id=other_core, device_id_type=MESH)
    for b in range(4):
        lines[pl.ds(b * 4, 4), :] = enc_ref[:, b * BLOCK : (b + 1) * BLOCK].astype(jnp.float32)
    enc64[pl.ds(pl.multiple_of(t * 16, 16), 16), :] = lines[...].astype(jnp.bfloat16)
    for copy in loads:
        copy.wait()
    pl.semaphore_wait(barrier, 13)

    def wait_bytes(sem, rows):
        wait_for(wq.at[0, pl.ds(0, rows)], sem)

    def z_first(c):
        own = piece(c, x, z)
        for k in (1, -1):
            remote(own, own, z_send.at[c], z_near.at[c], at_z(k)).start()

    def z_second(c):
        wait_bytes(z_near.at[c], 2 * SHARD)
        up = piece(c, x, (z + 3) % 4, HALF, HALF)
        remote(up, up, z_send.at[c], z_far.at[c], at_z(1)).start()
        down = piece(c, x, (z + 1) % 4, 0, HALF)
        remote(down, down, z_send.at[c], z_far.at[c], at_z(-1)).start()

    def x_first(h, j):
        own = piece(h, x, (z + j) % 4)
        for k in (1, -1):
            remote(own, own, x_send.at[h], x_near.at[j, h], at_x(k)).start()

    def x_second(h, j):
        wait_bytes(x_near.at[j, h], 2 * SHARD)
        up = piece(h, (x + 3) % 4, (z + j) % 4, HALF, HALF)
        remote(up, up, x_send.at[h], x_far.at[j, h], at_x(1)).start()
        down = piece(h, (x + 1) % 4, (z + j) % 4, 0, HALF)
        remote(down, down, x_send.at[h], x_far.at[j, h], at_x(-1)).start()

    own16 = rows_of(enc64, t, 16)
    for k in range(1, 4):
        remote(own16, own16, e_send.at[0], e_recv.at[0], at_t(k)).start()
    z_first(0)
    z_first(1)
    x_first(0, 0)
    x_first(1, 0)

    def enc_x():
        wait_for(enc64.at[pl.ds(0, 48)], e_recv.at[0])
        moved = regroup(enc64[...]).astype(jnp.bfloat16)
        for b in range(4):
            encx[b] = moved[b * 16 : (b + 1) * 16]
        enc[pl.ds(pl.multiple_of(pipe * 64 + x * 16, 16), 16), :] = encx[x]
        for k in range(1, 4):
            remote(
                encx.at[(x + k) % 4],
                enc.at[pl.ds(pl.multiple_of(pipe * 64 + x * 16, 16), 16)],
                e_send.at[1], e_recv.at[1], at_x(k),
            ).start()

    def enc_y():
        wait_for(enc.at[pl.ds(0, 48)], e_recv.at[1])
        mine = rows_of(enc, pipe, 64)
        for k in range(1, 4):
            remote(mine, mine, e_send.at[2], e_recv.at[2], at_y(k)).start()

    def enc_core():
        wait_for(enc.at[pl.ds(0, 192)], e_recv.at[2])
        for k in range(4):
            mine = rows_of(enc, k * 2 + core, 64)
            remote(mine, mine, e_send.at[3], e_recv.at[3], other_core).start()

    def norm():
        x_load.wait()
        total = jnp.zeros((ROWS, 1), jnp.float32)
        for b in range(4):
            block = xv[:, b * BLOCK : (b + 1) * BLOCK].astype(jnp.float32)
            total += jnp.sum(block * block, axis=1, keepdims=True)
        scale = lax.rsqrt(total / D + EPSILON)
        inv[...] = jnp.broadcast_to(scale, (ROWS, 128))
        for b in range(4):
            cols = slice(b * BLOCK, (b + 1) * BLOCK)
            normed = xv[:, cols].astype(jnp.float32) * scale
            hid[:, cols] = (normed * gain_ref[:, cols]).astype(jnp.bfloat16)

    def share(m, h):
        wait_bytes(z_far.at[2 + 2 * m + h], SHARD)
        rows = jnp.dot(enc[...], wkv[m, h], preferred_element_type=jnp.float32).astype(jnp.bfloat16)
        for p in range(8):
            for b in range(4):
                part[m, h, b, pl.ds(p * 16, 16), :] = rows[p * 64 + b * 16 : p * 64 + (b + 1) * 16]
        for k in range(1, 4):
            remote(
                part.at[m, h, (x + k) % 4], part_in.at[m, h, x],
                p_send.at[m, h], p_recv.at[m, h], at_x(k),
            ).start()

    def combine(m, h):
        arrived(part_in.at[m, h], p_recv.at[m, h])
        total = part[m, h, x].astype(jnp.float32)
        for k in range(1, 4):
            total += part_in[m, h, (x + k) % 4].astype(jnp.float32)
        kv[m, h] = total.astype(jnp.bfloat16)

    scale = 1.0 / math.sqrt(HEAD_DIM)

    def spread(m, h, grad):
        dkv[m, h, x] = grad.astype(jnp.bfloat16)
        mine = dkv.at[m, h, x]
        for k in range(1, 4):
            remote(mine, mine, k_send.at[m, h], k_recv.at[m, h], at_x(k)).start()

    def queries(h):
        for j in range(4):
            wait_bytes(x_far.at[j, h], SHARD)
        total = jnp.zeros((ROWS, HEAD_DIM), jnp.float32)

        def add(k, total):
            at = pl.ds(pl.multiple_of(k * BLOCK, BLOCK), BLOCK)
            return total + jnp.dot(hid[:, at], wq[h, at, :], preferred_element_type=jnp.float32)

        qb[h] = lax.fori_loop(0, 4, add, total).astype(jnp.bfloat16)

    def soften(h):
        expo = jnp.exp(dot_nt(qb[h], kv[0, h]) * scale)
        soft = expo / jnp.sum(expo, axis=1, keepdims=True)
        probs[h] = soft
        head = hg[:, h * HEAD_DIM : (h + 1) * HEAD_DIM]
        spread(1, h, dot_tn(soft.astype(jnp.bfloat16), head))

    def attend(h):
        soft = probs[h]
        prob_grad = dot_nt(hg[:, h * HEAD_DIM : (h + 1) * HEAD_DIM], kv[1, h])
        mean = jnp.sum(prob_grad * soft, axis=1, keepdims=True)
        score_grad = (soft * (prob_grad - mean) * scale).astype(jnp.bfloat16)
        spread(0, h, dot_tn(score_grad, qb[h]))
        dq[h] = jnp.dot(score_grad, kv[0, h], preferred_element_type=jnp.float32).astype(
            jnp.bfloat16
        )

    def term(m, h, cols):
        left = dkv[m, h].reshape(4 * ROWS, HEAD_DIM)
        return dot_nt(left, wkv[m, h, cols, :])

    def early_encoder():
        arrived(dkv.at[1, 0], k_recv.at[1, 0])
        arrived(dkv.at[1, 1], k_recv.at[1, 1])

        @pl.loop(0, 4)
        def _(b):
            at = pl.ds(pl.multiple_of(b * HEAD_DIM, HEAD_DIM), HEAD_DIM)
            de[:, at] = term(1, 0, at)

    z_second(0)
    z_first(2)
    x_first(0, 1)
    x_first(0, 3)
    enc_x()
    norm()
    x_second(0, 0)
    x_second(1, 0)

    z_second(1)
    z_first(3)
    x_first(1, 1)
    x_first(1, 3)
    enc_y()
    wait_bytes(z_far.at[0], SHARD)
    x_first(0, 2)
    x_second(0, 1)
    x_second(0, 3)

    z_second(2)
    z_first(4)
    enc_core()
    wait_bytes(z_far.at[1], SHARD)
    x_first(1, 2)
    x_second(0, 2)
    x_second(1, 1)
    x_second(1, 3)

    z_second(3)
    z_first(5)
    x_second(1, 2)
    wait_for(enc.at[pl.ds(0, 256)], e_recv.at[3])
    share(0, 0)
    queries(0)
    queries(1)
    hg_load.wait()

    z_second(4)
    combine(0, 0)
    soften(0)

    z_second(5)
    share(0, 1)
    share(1, 0)
    combine(0, 1)
    soften(1)
    combine(1, 0)
    attend(0)

    share(1, 1)
    early_encoder()
    combine(1, 1)
    attend(1)

    note[...] = jnp.zeros_like(note)

    def hidden_block(j):
        at = pl.ds(pl.multiple_of(j * BLOCK, BLOCK), BLOCK)
        low = (dot_nt(dq[0], wq[0, at, :]) + dot_nt(dq[1], wq[1, at, :])).astype(jnp.bfloat16)
        hp[j] = low
        product = low.astype(jnp.float32) * (xv[:, at].astype(jnp.float32) * inv[:, :1])
        gain = jnp.sum(product, axis=0, keepdims=True)
        product *= gain_ref[:, at]
        folded = product[:, :128]
        for b in range(8):
            gx[x, j, pl.ds(b, 1)] = gain[:, b * 128 : (b + 1) * 128]
            if b:
                folded += product[:, b * 128 : (b + 1) * 128]
        return folded

    def hidden_step(k, folded):
        j = (t + k) % 4
        folded += hidden_block(j)
        remote(hp.at[j], hp_in.at[t], h_send.at[0], h_recv.at[0], at_t(k)).start()
        return folded

    folded = lax.fori_loop(1, 4, hidden_step, jnp.zeros((ROWS, 128), jnp.float32))
    folded += hidden_block(t)
    for k in range(1, 4):
        remote(gx.at[x], gx.at[x], g_send.at[0], g_recv.at[0], at_x(k)).start()
    row = jnp.sum(folded.T, axis=0, keepdims=True)

    for h in range(HEADS_HERE):
        arrived(dkv.at[0, h], k_recv.at[0, h])

    def seq_rows(s, k, c):
        return pl.ds(pl.multiple_of(s * ROWS + (k * 2 + c) * 16, 16), 16)

    halves = [slice(0, COLS), slice(COLS, 2 * COLS)]
    for b, cols in enumerate(halves):
        for lane in (cols.start, cols.start + HEAD_DIM):
            at = slice(lane, lane + HEAD_DIM)
            de[:, at] += term(1, 1, at) + term(0, 0, at) + term(0, 1, at)
        for s in range(4):
            for k in range(4):
                de1[b, k, s] = de[seq_rows(s, k, 1 - core), cols].astype(jnp.bfloat16)
        remote(de1.at[b], de1_in.at[b], d_send.at[0, b], d_recv.at[0, b], other_core).start()

    arrived(gx, g_recv.at[0])
    for j in range(4):
        note[j, pl.ds(0, 1)] = row
        note[j, pl.ds(8, 8)] = gx[0, j] + gx[1, j] + gx[2, j] + gx[3, j]
    for k in range(1, 4):
        remote(
            note.at[(t + k) % 4], note_in.at[t], i_send.at[0], i_recv.at[0], at_t(k)
        ).start()

    for b, cols in enumerate(halves):
        wait_for(de1_in.at[b], d_recv.at[0, b])
        for k in range(1, 4):
            to = (y + k) % 4
            for s in range(4):
                de2[b, to, s] = (
                    de[seq_rows(s, to, core), cols] + de1_in[b, to, s].astype(jnp.float32)
                ).astype(jnp.bfloat16)
            remote(
                de2.at[b, to], de2_in.at[b, y], d_send.at[1, b], d_recv.at[1, b], at_y(k)
            ).start()

    for b, cols in enumerate(halves):
        arrived(de2_in.at[b], d_recv.at[1, b])
        for s in range(4):
            total = de[seq_rows(s, y, core), cols] + de1_in[b, y, s].astype(jnp.float32)
            for k in range(1, 4):
                total += de2_in[b, (y + k) % 4, s].astype(jnp.float32)
            dex[s, :, cols] = total.astype(jnp.bfloat16)
    for k in range(1, 4):
        remote(dex.at[(x + k) % 4], dex_in.at[x], d_send.at[2, 0], d_recv.at[2, 0], at_x(k)).start()

    arrived(note_in, i_recv.at[0])
    note_in[t] = note[t]
    noted = note_in[0] + note_in[1] + note_in[2] + note_in[3]
    gz[z] = noted[8:]
    for k in range(1, 4):
        remote(gz.at[z], gz.at[z], g_send.at[1], g_recv.at[1], at_z(k)).start()
    mean = jnp.broadcast_to(noted[:1] / D, (128, 128)).T[:, :1]

    arrived(dex_in, d_recv.at[2, 0])
    dex_in[x] = dex[x]
    stacked = jnp.concatenate([dex_in[b] for b in range(4)], axis=0)
    moved = regroup(stacked).astype(jnp.bfloat16)
    for b in range(4):
        de3[b] = moved[b * 16 : (b + 1) * 16]
    for k in range(1, 4):
        remote(
            de3.at[(t + k) % 4], de3_in.at[t], d_send.at[2, 1], d_recv.at[2, 1], at_t(k)
        ).start()

    og_load.wait()
    at = pl.ds(pl.multiple_of(t * BLOCK, BLOCK), BLOCK)
    scale_col = inv[:, :1]
    normed = xv[:, at].astype(jnp.float32) * scale_col
    arrived(hp_in, h_recv.at[0])
    hidden_grad = hp[t].astype(jnp.float32)
    for k in range(1, 4):
        hidden_grad += hp_in[(t + k) % 4].astype(jnp.float32)
    normed_grad = hidden_grad * gain_ref[:, at]
    ig_ref[0] = (
        og[...].astype(jnp.float32) + scale_col * (normed_grad - normed * mean)
    ).astype(jnp.bfloat16)

    arrived(gz, g_recv.at[1])
    gains = gz[0] + gz[1] + gz[2] + gz[3]
    for b in range(8):
        gg_ref[:, b * 128 : (b + 1) * 128] = gains[b : b + 1]

    arrived(de3_in, d_recv.at[2, 1])
    summed = de3[t].astype(jnp.float32)
    for k in range(1, 4):
        summed += de3_in[(t + k) % 4].astype(jnp.float32)
    lines[...] = summed
    for b in range(4):
        eg_ref[:, b * BLOCK : (b + 1) * BLOCK] = lines[pl.ds(b * 4, 4), :]

    for c in range(6):
        wait_bytes(z_send.at[c], 3 * SHARD)
    for h in range(HEADS_HERE):
        wait_bytes(x_send.at[h], 12 * SHARD)
        for m in range(2):
            arrived(part.at[m, h], p_send.at[m, h])
            arrived(dkv.at[m, h], k_send.at[m, h])
    wait_for(enc64.at[pl.ds(0, 48)], e_send.at[0])
    wait_for(enc.at[pl.ds(0, 48)], e_send.at[1])
    wait_for(enc.at[pl.ds(0, 192)], e_send.at[2])
    wait_for(enc.at[pl.ds(0, 256)], e_send.at[3])
    arrived(hp, h_send.at[0])
    arrived(note, i_send.at[0])
    for b in range(2):
        wait_for(de1.at[b], d_send.at[0, b])
        arrived(de2.at[b], d_send.at[1, b])
    arrived(dex, d_send.at[2, 0])
    arrived(de3, d_send.at[2, 1])
    arrived(gx, g_send.at[0])
    arrived(gz, g_send.at[1])


def shards(
    section_input, out_grad, head_grad, encoder, norm_gain, query_weight, key_weight, value_weight
):
    low, f32 = jnp.bfloat16, jnp.float32
    hbm = pl.BlockSpec(memory_space=pl.ANY)
    vmem = pl.BlockSpec(memory_space=pltpu.VMEM)
    dma = pltpu.SemaphoreType.DMA
    two = (2, HEADS_HERE)
    return pl.pallas_call(
        kernel,
        out_shape=(
            jax.ShapeDtypeStruct((1, ROWS, BLOCK), low),
            jax.ShapeDtypeStruct((4, D), f32),
            jax.ShapeDtypeStruct((1, BLOCK), f32),
        ),
        in_specs=[hbm, hbm, hbm, vmem, vmem, hbm, hbm, hbm],
        out_specs=(vmem, vmem, vmem),
        scratch_shapes=[
            pltpu.VMEM((HEADS_HERE, D, HEAD_DIM), low),
            pltpu.VMEM(two + (BLOCK, HEAD_DIM), low),
            pltpu.VMEM((ROWS, D), low),
            pltpu.VMEM((ROWS, BLOCK), low),
            pltpu.VMEM((ROWS, COLS), low),
            pltpu.VMEM((16, BLOCK), f32),
            pltpu.VMEM((64, BLOCK), low),
            pltpu.VMEM((4, 16, BLOCK), low),
            pltpu.VMEM((4 * ROWS, BLOCK), low),
            pltpu.VMEM((ROWS, D), low),
            pltpu.VMEM((ROWS, 128), f32),
            pltpu.VMEM(two + (4, ROWS, HEAD_DIM), low),
            pltpu.VMEM(two + (4, ROWS, HEAD_DIM), low),
            pltpu.VMEM(two + (ROWS, HEAD_DIM), low),
            pltpu.VMEM((HEADS_HERE, ROWS, HEAD_DIM), low),
            pltpu.VMEM((HEADS_HERE, ROWS, ROWS), f32),
            pltpu.VMEM((HEADS_HERE, ROWS, HEAD_DIM), low),
            pltpu.VMEM(two + (4, ROWS, HEAD_DIM), low),
            pltpu.VMEM((4, ROWS, BLOCK), low),
            pltpu.VMEM((4, ROWS, BLOCK), low),
            pltpu.VMEM((4, 16, 128), f32),
            pltpu.VMEM((4, 16, 128), f32),
            pltpu.VMEM((4 * ROWS, BLOCK), f32),
            pltpu.VMEM((2, 4, 4, 16, COLS), low),
            pltpu.VMEM((2, 4, 4, 16, COLS), low),
            pltpu.VMEM((2, 4, 4, 16, COLS), low),
            pltpu.VMEM((2, 4, 4, 16, COLS), low),
            pltpu.VMEM((4, 16, BLOCK), low),
            pltpu.VMEM((4, 16, BLOCK), low),
            pltpu.VMEM((4, 16, BLOCK), low),
            pltpu.VMEM((4, 16, BLOCK), low),
            pltpu.VMEM((4, 8, 128), f32),
            pltpu.VMEM((4, 4, 8, 128), f32),
            dma((10,)),
            dma((6,)),
            dma((HEADS_HERE,)),
            dma((6,)),
            dma((6,)),
            dma((4, HEADS_HERE)),
            dma((4, HEADS_HERE)),
            dma(two),
            dma(two),
            dma(two),
            dma(two),
            dma((4,)),
            dma((4,)),
            dma((1,)),
            dma((1,)),
            dma((1,)),
            dma((1,)),
            dma((3, 2)),
            dma((3, 2)),
            dma((2,)),
            dma((2,)),
        ],
        compiler_params=pltpu.CompilerParams(
            collective_id=0, has_side_effects=True, vmem_limit_bytes=60 * 1024 * 1024
        ),
        cost_estimate=pl.CostEstimate(
            flops=6 * 2 * ROWS * D * COLS, bytes_accessed=4 * 1024 * 1024, transcendentals=0
        ),
    )(
        section_input, out_grad, head_grad, encoder, norm_gain,
        query_weight, key_weight, value_weight,
    )


def solution(mesh):
    placed = (
        P("pipe", "dp", None),
        P("pipe", "dp", None),
        P("pipe", "dp", "tensor"),
        P(("dp", "pipe", "tensor"), None),
        P("pipe", None),
        P("pipe", "dp", "tensor"),
        P("pipe", "dp", "tensor"),
        P("pipe", "dp", "tensor"),
    )
    return jax.shard_map(
        shards,
        mesh=mesh,
        in_specs=placed,
        out_specs=(
            P("pipe", "dp", "tensor"),
            P(("dp", "pipe", "tensor"), None),
            P("pipe", "tensor"),
        ),
        check_vma=False,
    )
```

time: 183 us -> 172 us (0.940); the launches traced: 180 us -> 171 us
  Pallas kernels: 174 us -> 168 us
  local copies, waits for them, and re-layouts: 5.14 us -> 2.98 us
    pallas_call x1, Pallas kernels: 174 us -> 168 us  [shards(): pl.pallas_call(kernel, out_shape=(jax.ShapeDtypeStruct((1, ROWS, BLOCK),...]
    reshape x2 -> x0, local copies, waits for them, and re-layouts: 2.87 us -> none  [the longest x1 1.49 us: shards(): enc_grad = enc_grad.reshape(4, 4, BLOCK).transpose(1, 0, 2).reshape(4, D)]
where the time goes in v3:
time: 172 us; the launch traced here: 171 us
  Pallas kernels  168 us (98%)
  local copies, waits for them, and re-layouts  2.98 us (2%)
    pallas_call x1, Pallas kernels, shards(): pl.pallas_call(kernel, out_shape=(jax.ShapeDtypeStruct((1, ROWS, BLOCK),...  168 us

profile of v3, /device:TPU:24, one launch (start us, length us, event | category | flops | bytes accessed | tf_op | source)
XLA Modules:
  0.0 171.5 jit_solution(1225847979549295302)
XLA Ops:
  0.6 167.8 %shard_map.103 = (bf16[1,128,1024]{2,1,0:T(8,128)(2,1)}, f32[4,4096]{1,0:T(4,128)}, f32[1,1024]{1,0:T(1,128)}) custom-call(bf16[1,128,4096]{2,1,0:T(8,128)(2,1)} %x_hbm.1, bf16[1,128,4096]{2,1,0:T(8,128)(2,1)} %og_hbm.1, bf16[1,128,512]{2,1,0:T(8,128)(2,1)} %hg_hbm.1, bf16[4,4096]{1,0:T(4,128)(2,1)} %enc_ref.1, f32[1,4096]{1,0:T(1,128)} %gain_ref.1, ...), custom_call_target="tpu_custom_call" | custom-call | flops 3221225472 | bytes 4194304 | tf_op jit(solution)/shard_map/pallas_call | solution.py:464
  168.5 0.0 copy-start
  168.5 1.7 copy.14
  170.2 0.0 copy-done
  170.2 0.0 copy-start.1
  170.2 0.6 copy.15
  170.8 0.0 copy-done.1
  170.9 0.6 copy.16
Async XLA Ops:
  168.5 1.7 copy-start
  170.2 0.7 copy-start.1

commit v4 on v3

--- a/solution.py
+++ b/solution.py
@@ -17,6 +17,11 @@
 BLOCK = 1024
 EPSILON = 1e-06
 MESH = pl.DeviceIdType.MESH
+QUARTER = SHARD // 4
+PIECES = [
+    (0, 0, 0, SHARD), (0, 1, 0, SHARD), (1, 0, 0, SHARD), (1, 1, 0, SHARD), (2, 0, 0, SHARD),
+    (2, 1, 0, HALF), (2, 1, HALF, HALF),
+]
 
 
 def dot_nt(left, right):
@@ -43,7 +48,7 @@
     x_hbm, og_hbm, hg_hbm, enc_ref, gain_ref, wq_hbm, wk_hbm, wv_hbm,
     ig_ref, eg_ref, gg_ref,
     wq, wkv, xv, og, hg, lines, enc64, encx, enc, hid, inv, part, part_in, kv, qb, probs, dq, dkv,
-    hp, hp_in, note, note_in, de, de1, de1_in, de2, de2_in, dex, dex_in, de3, de3_in, gz, gx,
+    hp, hp_in, note, note_in, de, de1, de1_in, de2, de2_in, de3, de3_in, gz, gz_in, gx,
     local, z_send, x_send, z_near, z_far, x_near, x_far, p_send, p_recv, k_send, k_recv,
     e_send, e_recv, h_send, h_recv, i_send, i_recv, d_send, d_recv, g_send, g_recv,
 ):
@@ -65,6 +70,14 @@
     def at_t(k):
         return (dp, pipe, (t + k) % 4)
 
+    def at_line(k):
+        to = (z * 4 + t + k) % 16
+        return (x * 4 + to // 4, pipe, to % 4)
+
+    def at_plane(k):
+        to = (x * 4 + t + k) % 16
+        return (to // 4 * 4 + z, pipe, to % 4)
+
     other_core = (dp, y * 2 + 1 - core, t)
 
     def remote(src, dst, send, recv, peer):
@@ -82,39 +95,42 @@
     def arrived(ref, sem):
         wait_for(ref.at[pl.ds(0, 3)], sem)
 
-    def piece(c, xx, zz, start=0, rows=SHARD):
-        m, h = c // 2, c % 2
+    def piece(c, xx, zz, start=0, rows=None):
+        m, h, first_row, count = PIECES[c]
+        start, rows = start + first_row, rows or count
         if m == 0:
             first = (xx * 4 + zz) * SHARD + start
-            return wq.at[h, pl.ds(pl.multiple_of(first, HALF), rows)]
-        return wkv.at[m - 1, h, pl.ds(pl.multiple_of(zz * SHARD + start, HALF), rows)]
+            return wq.at[h, pl.ds(pl.multiple_of(first, QUARTER), rows)]
+        return wkv.at[m - 1, h, pl.ds(pl.multiple_of(zz * SHARD + start, QUARTER), rows)]
 
     sources = (wq_hbm, wk_hbm, wv_hbm)
     loads = [
         pltpu.make_async_copy(
-            sources[c // 2].at[0, :, pl.ds(c % 2 * HEAD_DIM, HEAD_DIM)], piece(c, x, z), local.at[c]
+            sources[m].at[0, pl.ds(start, rows), pl.ds(h * HEAD_DIM, HEAD_DIM)],
+            piece(c, x, z), local.at[c],
         )
-        for c in range(6)
+        for c, (m, h, start, rows) in enumerate(PIECES)
     ]
-    x_load = pltpu.make_async_copy(x_hbm.at[0], xv, local.at[7])
-    hg_load = pltpu.make_async_copy(hg_hbm.at[0], hg, local.at[8])
+    x_load = pltpu.make_async_copy(x_hbm.at[0], xv, local.at[8])
+    hg_load = pltpu.make_async_copy(hg_hbm.at[0], hg, local.at[9])
     og_load = pltpu.make_async_copy(
-        og_hbm.at[0, :, pl.ds(pl.multiple_of(t * BLOCK, BLOCK), BLOCK)], og, local.at[9]
+        og_hbm.at[0, :, pl.ds(pl.multiple_of(t * BLOCK, BLOCK), BLOCK)], og, local.at[10]
     )
     for copy in loads + [x_load, hg_load, og_load]:
         copy.start()
 
     barrier = pltpu.get_barrier_semaphore()
+    peers = [at_line(k) for k in range(1, 16)] + [other_core]
     for k in range(1, 4):
-        for peer in (at_z(k), at_x(k), at_y(k), at_t(k)):
-            pl.semaphore_signal(barrier, inc=1, device_id=peer, device_id_type=MESH)
-    pl.semaphore_signal(barrier, inc=1, device_id=other_core, device_id_type=MESH)
+        peers += [at_y(k)] + [((x + k) % 4 * 4 + z, pipe, b) for b in range(4)]
+    for peer in peers:
+        pl.semaphore_signal(barrier, inc=1, device_id=peer, device_id_type=MESH)
     for b in range(4):
         lines[pl.ds(b * 4, 4), :] = enc_ref[:, b * BLOCK : (b + 1) * BLOCK].astype(jnp.float32)
     enc64[pl.ds(pl.multiple_of(t * 16, 16), 16), :] = lines[...].astype(jnp.bfloat16)
     for copy in loads:
         copy.wait()
-    pl.semaphore_wait(barrier, 13)
+    pl.semaphore_wait(barrier, len(peers))
 
     def wait_bytes(sem, rows):
         wait_for(wq.at[0, pl.ds(0, rows)], sem)
@@ -125,10 +141,11 @@
             remote(own, own, z_send.at[c], z_near.at[c], at_z(k)).start()
 
     def z_second(c):
-        wait_bytes(z_near.at[c], 2 * SHARD)
-        up = piece(c, x, (z + 3) % 4, HALF, HALF)
+        rows = PIECES[c][3]
+        wait_bytes(z_near.at[c], 2 * rows)
+        up = piece(c, x, (z + 3) % 4, rows // 2, rows // 2)
         remote(up, up, z_send.at[c], z_far.at[c], at_z(1)).start()
-        down = piece(c, x, (z + 1) % 4, 0, HALF)
+        down = piece(c, x, (z + 1) % 4, 0, rows // 2)
         remote(down, down, z_send.at[c], z_far.at[c], at_z(-1)).start()
 
     def x_first(h, j):
@@ -190,7 +207,9 @@
             hid[:, cols] = (normed * gain_ref[:, cols]).astype(jnp.bfloat16)
 
     def share(m, h):
-        wait_bytes(z_far.at[2 + 2 * m + h], SHARD)
+        for c, (weight, head, _, rows) in enumerate(PIECES):
+            if (weight, head) == (m + 1, h):
+                wait_bytes(z_far.at[c], rows)
         rows = jnp.dot(enc[...], wkv[m, h], preferred_element_type=jnp.float32).astype(jnp.bfloat16)
         for p in range(8):
             for b in range(4):
@@ -287,6 +306,7 @@
 
     z_second(3)
     z_first(5)
+    z_first(6)
     x_second(1, 2)
     wait_for(enc.at[pl.ds(0, 256)], e_recv.at[3])
     share(0, 0)
@@ -300,18 +320,17 @@
 
     z_second(5)
     share(0, 1)
+    z_second(6)
     share(1, 0)
     combine(0, 1)
     soften(1)
+
+    share(1, 1)
     combine(1, 0)
     attend(0)
-
-    share(1, 1)
     early_encoder()
     combine(1, 1)
     attend(1)
-
-    note[...] = jnp.zeros_like(note)
 
     def hidden_block(j):
         at = pl.ds(pl.multiple_of(j * BLOCK, BLOCK), BLOCK)
@@ -338,6 +357,9 @@
     for k in range(1, 4):
         remote(gx.at[x], gx.at[x], g_send.at[0], g_recv.at[0], at_x(k)).start()
     row = jnp.sum(folded.T, axis=0, keepdims=True)
+    note[...] = jnp.broadcast_to(row, (8, 128))
+    for k in range(1, 4):
+        remote(note, note_in.at[t], i_send.at[0], i_recv.at[0], at_t(k)).start()
 
     for h in range(HEADS_HERE):
         arrived(dkv.at[0, h], k_recv.at[0, h])
@@ -357,11 +379,10 @@
 
     arrived(gx, g_recv.at[0])
     for j in range(4):
-        note[j, pl.ds(0, 1)] = row
-        note[j, pl.ds(8, 8)] = gx[0, j] + gx[1, j] + gx[2, j] + gx[3, j]
-    for k in range(1, 4):
+        gz[j] = gx[0, j] + gx[1, j] + gx[2, j] + gx[3, j]
+    for k in range(1, 16):
         remote(
-            note.at[(t + k) % 4], note_in.at[t], i_send.at[0], i_recv.at[0], at_t(k)
+            gz.at[(t + k) % 4], gz_in.at[z * 4 + t], g_send.at[1], g_recv.at[1], at_line(k)
         ).start()
 
     for b, cols in enumerate(halves):
@@ -376,39 +397,34 @@
                 de2.at[b, to], de2_in.at[b, y], d_send.at[1, b], d_recv.at[1, b], at_y(k)
             ).start()
 
+    quarters = [[] for _ in range(4)]
     for b, cols in enumerate(halves):
         arrived(de2_in.at[b], d_recv.at[1, b])
         for s in range(4):
             total = de[seq_rows(s, y, core), cols] + de1_in[b, y, s].astype(jnp.float32)
             for k in range(1, 4):
                 total += de2_in[b, (y + k) % 4, s].astype(jnp.float32)
-            dex[s, :, cols] = total.astype(jnp.bfloat16)
-    for k in range(1, 4):
-        remote(dex.at[(x + k) % 4], dex_in.at[x], d_send.at[2, 0], d_recv.at[2, 0], at_x(k)).start()
-
-    arrived(note_in, i_recv.at[0])
-    note_in[t] = note[t]
-    noted = note_in[0] + note_in[1] + note_in[2] + note_in[3]
-    gz[z] = noted[8:]
-    for k in range(1, 4):
-        remote(gz.at[z], gz.at[z], g_send.at[1], g_recv.at[1], at_z(k)).start()
-    mean = jnp.broadcast_to(noted[:1] / D, (128, 128)).T[:, :1]
-
-    arrived(dex_in, d_recv.at[2, 0])
-    dex_in[x] = dex[x]
-    stacked = jnp.concatenate([dex_in[b] for b in range(4)], axis=0)
+            low = total.astype(jnp.bfloat16)
+            quarters[s] += [low[:, :HEAD_DIM], low[:, HEAD_DIM:]]
+    stacked = jnp.concatenate([jnp.concatenate(q, axis=0) for q in quarters], axis=1)
     moved = regroup(stacked).astype(jnp.bfloat16)
-    for b in range(4):
-        de3[b] = moved[b * 16 : (b + 1) * 16]
-    for k in range(1, 4):
+    for s in range(4):
+        for b in range(4):
+            de3[s * 4 + b] = moved[b * 16 : (b + 1) * 16, s * HEAD_DIM : (s + 1) * HEAD_DIM]
+    for k in range(1, 16):
         remote(
-            de3.at[(t + k) % 4], de3_in.at[t], d_send.at[2, 1], d_recv.at[2, 1], at_t(k)
+            de3.at[(x * 4 + t + k) % 16], de3_in.at[x * 4 + t],
+            d_send.at[2, 0], d_recv.at[2, 0], at_plane(k),
         ).start()
 
     og_load.wait()
     at = pl.ds(pl.multiple_of(t * BLOCK, BLOCK), BLOCK)
     scale_col = inv[:, :1]
     normed = xv[:, at].astype(jnp.float32) * scale_col
+    arrived(note_in, i_recv.at[0])
+    note_in[t] = note[...]
+    noted = note_in[0] + note_in[1] + note_in[2] + note_in[3]
+    mean = jnp.broadcast_to(noted[:1] / D, (128, 128)).T[:, :1]
     arrived(hp_in, h_recv.at[0])
     hidden_grad = hp[t].astype(jnp.float32)
     for k in range(1, 4):
@@ -418,21 +434,29 @@
         og[...].astype(jnp.float32) + scale_col * (normed_grad - normed * mean)
     ).astype(jnp.bfloat16)
 
-    arrived(gz, g_recv.at[1])
-    gains = gz[0] + gz[1] + gz[2] + gz[3]
+    wait_for(gz_in.at[pl.ds(0, 15)], g_recv.at[1])
+    gz_in[z * 4 + t] = gz[t]
+    gains = gz_in[0]
+    for k in range(1, 16):
+        gains += gz_in[k]
     for b in range(8):
         gg_ref[:, b * 128 : (b + 1) * 128] = gains[b : b + 1]
 
-    arrived(de3_in, d_recv.at[2, 1])
-    summed = de3[t].astype(jnp.float32)
-    for k in range(1, 4):
-        summed += de3_in[(t + k) % 4].astype(jnp.float32)
-    lines[...] = summed
+    wait_for(de3_in.at[pl.ds(0, 15)], d_recv.at[2, 0])
+    de3_in[x * 4 + t] = de3[x * 4 + t]
     for b in range(4):
-        eg_ref[:, b * BLOCK : (b + 1) * BLOCK] = lines[pl.ds(b * 4, 4), :]
-
-    for c in range(6):
-        wait_bytes(z_send.at[c], 3 * SHARD)
+        summed = de3_in[b * 4].astype(jnp.float32)
+        for k in range(1, 4):
+            summed += de3_in[b * 4 + k].astype(jnp.float32)
+        lines[:, b * HEAD_DIM : (b + 1) * HEAD_DIM] = summed
+    for b in range(4):
+        for k in range(4):
+            eg_ref[:, b * BLOCK + k * HEAD_DIM : b * BLOCK + (k + 1) * HEAD_DIM] = lines[
+                pl.ds(k * 4, 4), b * HEAD_DIM : (b + 1) * HEAD_DIM
+            ]
+
+    for c in range(len(PIECES)):
+        wait_bytes(z_send.at[c], 3 * PIECES[c][3])
     for h in range(HEADS_HERE):
         wait_bytes(x_send.at[h], 12 * SHARD)
         for m in range(2):
@@ -443,14 +467,13 @@
     wait_for(enc.at[pl.ds(0, 192)], e_send.at[2])
     wait_for(enc.at[pl.ds(0, 256)], e_send.at[3])
     arrived(hp, h_send.at[0])
-    arrived(note, i_send.at[0])
+    arrived(note_in, i_send.at[0])
     for b in range(2):
         wait_for(de1.at[b], d_send.at[0, b])
         arrived(de2.at[b], d_send.at[1, b])
-    arrived(dex, d_send.at[2, 0])
-    arrived(de3, d_send.at[2, 1])
+    wait_for(de3.at[pl.ds(0, 15)], d_send.at[2, 0])
     arrived(gx, g_send.at[0])
-    arrived(gz, g_send.at[1])
+    wait_for(gz_in.at[pl.ds(0, 15)], g_send.at[1])
 
 
 def shards(
@@ -464,9 +487,9 @@
     return pl.pallas_call(
         kernel,
         out_shape=(
-            jax.ShapeDtypeStruct((1, ROWS, BLOCK), low),
-            jax.ShapeDtypeStruct((4, D), f32),
-            jax.ShapeDtypeStruct((1, BLOCK), f32),
+            pltpu.VMEM((1, ROWS, BLOCK), low),
+            pltpu.VMEM((4, D), f32),
+            pltpu.VMEM((1, BLOCK), f32),
         ),
         in_specs=[hbm, hbm, hbm, vmem, vmem, hbm, hbm, hbm],
         out_specs=(vmem, vmem, vmem),
@@ -491,24 +514,23 @@
             pltpu.VMEM(two + (4, ROWS, HEAD_DIM), low),
             pltpu.VMEM((4, ROWS, BLOCK), low),
             pltpu.VMEM((4, ROWS, BLOCK), low),
-            pltpu.VMEM((4, 16, 128), f32),
-            pltpu.VMEM((4, 16, 128), f32),
+            pltpu.VMEM((8, 128), f32),
+            pltpu.VMEM((4, 8, 128), f32),
             pltpu.VMEM((4 * ROWS, BLOCK), f32),
             pltpu.VMEM((2, 4, 4, 16, COLS), low),
             pltpu.VMEM((2, 4, 4, 16, COLS), low),
             pltpu.VMEM((2, 4, 4, 16, COLS), low),
             pltpu.VMEM((2, 4, 4, 16, COLS), low),
-            pltpu.VMEM((4, 16, BLOCK), low),
-            pltpu.VMEM((4, 16, BLOCK), low),
-            pltpu.VMEM((4, 16, BLOCK), low),
-            pltpu.VMEM((4, 16, BLOCK), low),
+            pltpu.VMEM((16, 16, HEAD_DIM), low),
+            pltpu.VMEM((16, 16, HEAD_DIM), low),
             pltpu.VMEM((4, 8, 128), f32),
+            pltpu.VMEM((16, 8, 128), f32),
             pltpu.VMEM((4, 4, 8, 128), f32),
-            dma((10,)),
-            dma((6,)),
+            dma((11,)),
+            dma((len(PIECES),)),
             dma((HEADS_HERE,)),
-            dma((6,)),
-            dma((6,)),
+            dma((len(PIECES),)),
+            dma((len(PIECES),)),
             dma((4, HEADS_HERE)),
             dma((4, HEADS_HERE)),
             dma(two),

time: 172 us -> 165 us (0.959); the launches traced: 171 us -> 162 us
  Pallas kernels: 168 us -> 160 us
    pallas_call x1, Pallas kernels: 168 us -> 160 us  [shards(): pl.pallas_call(kernel, out_shape=(pltpu.VMEM((1, ROWS, BLOCK), low), pltp...]
where the time goes in v4:
time: 165 us; the launch traced here: 162 us
  Pallas kernels  160 us (97%)
  local copies, waits for them, and re-layouts  1.93 us (1%)
    pallas_call x1, Pallas kernels, shards(): pl.pallas_call(kernel, out_shape=(pltpu.VMEM((1, ROWS, BLOCK), low), pltp...  160 us

profile of v4, /device:TPU:24, one launch (start us, length us, event | category | flops | bytes accessed | tf_op | source)
XLA Modules:
  0.0 162.4 jit_solution(4012735527103433654)
XLA Ops:
  0.6 159.9 %shard_map.103 = (bf16[1,128,1024]{2,1,0:T(8,128)(2,1)S(1)}, f32[4,4096]{1,0:T(4,128)S(1)}, f32[1,1024]{1,0:T(1,128)S(1)}) custom-call(bf16[1,128,4096]{2,1,0:T(8,128)(2,1)} %x_hbm.1, bf16[1,128,4096]{2,1,0:T(8,128)(2,1)} %og_hbm.1, bf16[1,128,512]{2,1,0:T(8,128)(2,1)} %hg_hbm.1, bf16[4,4096]{1,0:T(4,128)(2,1)} %enc_ref.1, f32[1,4096]{1,0:T(1,128)} %gain_ref.1, ...), custom_call_target="tpu_custom_call" | custom-call | flops 3221225472 | bytes 4194304 | tf_op jit(solution)/shard_map/pallas_call | solution.py:487
  160.5 0.7 copy.14
  161.2 0.6 copy.16
  161.8 0.6 copy.15

commit v5 on v4

--- a/solution.py
+++ b/solution.py
@@ -48,7 +48,7 @@
     x_hbm, og_hbm, hg_hbm, enc_ref, gain_ref, wq_hbm, wk_hbm, wv_hbm,
     ig_ref, eg_ref, gg_ref,
     wq, wkv, xv, og, hg, lines, enc64, encx, enc, hid, inv, part, part_in, kv, qb, probs, dq, dkv,
-    hp, hp_in, note, note_in, de, de1, de1_in, de2, de2_in, de3, de3_in, gz, gz_in, gx,
+    hp, hp_in, hp_out, note, note_in, de, de1, de1_in, de2, de2_in, de3, de3_in, gz, gx,
     local, z_send, x_send, z_near, z_far, x_near, x_far, p_send, p_recv, k_send, k_recv,
     e_send, e_recv, h_send, h_recv, i_send, i_recv, d_send, d_recv, g_send, g_recv,
 ):
@@ -69,10 +69,6 @@
 
     def at_t(k):
         return (dp, pipe, (t + k) % 4)
-
-    def at_line(k):
-        to = (z * 4 + t + k) % 16
-        return (x * 4 + to // 4, pipe, to % 4)
 
     def at_plane(k):
         to = (x * 4 + t + k) % 16
@@ -120,9 +116,9 @@
         copy.start()
 
     barrier = pltpu.get_barrier_semaphore()
-    peers = [at_line(k) for k in range(1, 16)] + [other_core]
+    peers = [other_core]
     for k in range(1, 4):
-        peers += [at_y(k)] + [((x + k) % 4 * 4 + z, pipe, b) for b in range(4)]
+        peers += [at_z(k), at_t(k), at_y(k)] + [((x + k) % 4 * 4 + z, pipe, b) for b in range(4)]
     for peer in peers:
         pl.semaphore_signal(barrier, inc=1, device_id=peer, device_id_type=MESH)
     for b in range(4):
@@ -267,14 +263,18 @@
         left = dkv[m, h].reshape(4 * ROWS, HEAD_DIM)
         return dot_nt(left, wkv[m, h, cols, :])
 
+    tiles = [slice(b * HEAD_DIM, (b + 1) * HEAD_DIM) for b in range(4)]
+
     def early_encoder():
         arrived(dkv.at[1, 0], k_recv.at[1, 0])
         arrived(dkv.at[1, 1], k_recv.at[1, 1])
-
-        @pl.loop(0, 4)
-        def _(b):
-            at = pl.ds(pl.multiple_of(b * HEAD_DIM, HEAD_DIM), HEAD_DIM)
-            de[:, at] = term(1, 0, at)
+        for at in tiles:
+            de[:, at] = term(1, 0, at) + term(1, 1, at)
+
+    def late_encoder():
+        arrived(dkv.at[0, 0], k_recv.at[0, 0])
+        for at in tiles:
+            de[:, at] += term(0, 0, at)
 
     z_second(0)
     z_first(2)
@@ -300,13 +300,13 @@
     enc_core()
     wait_bytes(z_far.at[1], SHARD)
     x_first(1, 2)
+
+    z_second(3)
+    z_first(5)
+    z_first(6)
     x_second(0, 2)
     x_second(1, 1)
     x_second(1, 3)
-
-    z_second(3)
-    z_first(5)
-    z_first(6)
     x_second(1, 2)
     wait_for(enc.at[pl.ds(0, 256)], e_recv.at[3])
     share(0, 0)
@@ -328,7 +328,6 @@
     share(1, 1)
     combine(1, 0)
     attend(0)
-    early_encoder()
     combine(1, 1)
     attend(1)
 
@@ -341,28 +340,52 @@
         product *= gain_ref[:, at]
         folded = product[:, :128]
         for b in range(8):
-            gx[x, j, pl.ds(b, 1)] = gain[:, b * 128 : (b + 1) * 128]
+            note[j, pl.ds(8 + b, 1)] = gain[:, b * 128 : (b + 1) * 128]
             if b:
                 folded += product[:, b * 128 : (b + 1) * 128]
         return folded
 
-    def hidden_step(k, folded):
-        j = (t + k) % 4
-        folded += hidden_block(j)
-        remote(hp.at[j], hp_in.at[t], h_send.at[0], h_recv.at[0], at_t(k)).start()
-        return folded
-
-    folded = lax.fori_loop(1, 4, hidden_step, jnp.zeros((ROWS, 128), jnp.float32))
-    folded += hidden_block(t)
+    edge = jnp.logical_or(t == 0, t == 3)
+    inside = jnp.logical_not(edge)
+    mate = t + 1 - 2 * (t % 2)
+    outer = jnp.where(edge, 3 - t, 3 - mate)
+    nearer = 3 - t + 3 - mate - outer
+
+    def hand(block, slot, i, to):
+        remote(
+            block, hp_in.at[slot], h_send.at[i], h_recv.at[slot], (dp, pipe, to)
+        ).start()
+
+    folded = lax.fori_loop(
+        0, 4, lambda j, folded: folded + hidden_block(j), jnp.zeros((ROWS, 128), jnp.float32)
+    )
+
+    note[:, pl.ds(0, 8), :] = jnp.broadcast_to(
+        jnp.sum(folded.T, axis=0, keepdims=True)[None], (4, 8, 128)
+    )
     for k in range(1, 4):
-        remote(gx.at[x], gx.at[x], g_send.at[0], g_recv.at[0], at_x(k)).start()
-    row = jnp.sum(folded.T, axis=0, keepdims=True)
-    note[...] = jnp.broadcast_to(row, (8, 128))
+        remote(
+            note.at[(t + k) % 4], note_in.at[t], i_send.at[0], i_recv.at[0], at_t(k)
+        ).start()
+
+    @pl.when(edge)
+    def _():
+        for i, j in enumerate((outer, nearer)):
+            hand(hp.at[j], 2 + i, i, mate)
+
+    early_encoder()
+    late_encoder()
+    arrived(note_in, i_recv.at[0])
+    note_in[t] = note[t]
+    noted = note_in[0] + note_in[1] + note_in[2] + note_in[3]
+    mean = jnp.broadcast_to(noted[:1] / D, (128, 128)).T[:, :1]
+    gz[z] = noted[8:]
     for k in range(1, 4):
-        remote(note, note_in.at[t], i_send.at[0], i_recv.at[0], at_t(k)).start()
-
-    for h in range(HEADS_HERE):
-        arrived(dkv.at[0, h], k_recv.at[0, h])
+        remote(gz.at[z], gz.at[z], g_send.at[0], g_recv.at[0], at_z(k)).start()
+
+    hand(hp.at[mate], 0, 2, mate)
+
+    arrived(dkv.at[0, 1], k_recv.at[0, 1])
 
     def seq_rows(s, k, c):
         return pl.ds(pl.multiple_of(s * ROWS + (k * 2 + c) * 16, 16), 16)
@@ -371,19 +394,19 @@
     for b, cols in enumerate(halves):
         for lane in (cols.start, cols.start + HEAD_DIM):
             at = slice(lane, lane + HEAD_DIM)
-            de[:, at] += term(1, 1, at) + term(0, 0, at) + term(0, 1, at)
+            de[:, at] += term(0, 1, at)
         for s in range(4):
             for k in range(4):
                 de1[b, k, s] = de[seq_rows(s, k, 1 - core), cols].astype(jnp.bfloat16)
         remote(de1.at[b], de1_in.at[b], d_send.at[0, b], d_recv.at[0, b], other_core).start()
 
-    arrived(gx, g_recv.at[0])
-    for j in range(4):
-        gz[j] = gx[0, j] + gx[1, j] + gx[2, j] + gx[3, j]
-    for k in range(1, 16):
-        remote(
-            gz.at[(t + k) % 4], gz_in.at[z * 4 + t], g_send.at[1], g_recv.at[1], at_line(k)
-        ).start()
+    @pl.when(inside)
+    def _():
+        for i, j in enumerate((outer, nearer)):
+            wait_for(hp_in.at[2 + i], h_recv.at[2 + i])
+            both = hp[j].astype(jnp.float32) + hp_in[2 + i].astype(jnp.float32)
+            hp_out[i] = both.astype(jnp.bfloat16)
+            hand(hp_out.at[i], 1, i, j)
 
     for b, cols in enumerate(halves):
         wait_for(de1_in.at[b], d_recv.at[0, b])
@@ -417,28 +440,26 @@
             d_send.at[2, 0], d_recv.at[2, 0], at_plane(k),
         ).start()
 
+    arrived(gz, g_recv.at[0])
+    gx[x] = gz[0] + gz[1] + gz[2] + gz[3]
+    for k in range(1, 4):
+        remote(gx.at[x], gx.at[x], g_send.at[1], g_recv.at[1], at_x(k)).start()
+
     og_load.wait()
     at = pl.ds(pl.multiple_of(t * BLOCK, BLOCK), BLOCK)
     scale_col = inv[:, :1]
     normed = xv[:, at].astype(jnp.float32) * scale_col
-    arrived(note_in, i_recv.at[0])
-    note_in[t] = note[...]
-    noted = note_in[0] + note_in[1] + note_in[2] + note_in[3]
-    mean = jnp.broadcast_to(noted[:1] / D, (128, 128)).T[:, :1]
-    arrived(hp_in, h_recv.at[0])
     hidden_grad = hp[t].astype(jnp.float32)
-    for k in range(1, 4):
-        hidden_grad += hp_in[(t + k) % 4].astype(jnp.float32)
+    for k in range(2):
+        wait_for(hp_in.at[k], h_recv.at[k])
+        hidden_grad += hp_in[k].astype(jnp.float32)
     normed_grad = hidden_grad * gain_ref[:, at]
     ig_ref[0] = (
         og[...].astype(jnp.float32) + scale_col * (normed_grad - normed * mean)
     ).astype(jnp.bfloat16)
 
-    wait_for(gz_in.at[pl.ds(0, 15)], g_recv.at[1])
-    gz_in[z * 4 + t] = gz[t]
-    gains = gz_in[0]
-    for k in range(1, 16):
-        gains += gz_in[k]
+    arrived(gx, g_recv.at[1])
+    gains = gx[0] + gx[1] + gx[2] + gx[3]
     for b in range(8):
         gg_ref[:, b * 128 : (b + 1) * 128] = gains[b : b + 1]
 
@@ -466,14 +487,15 @@
     wait_for(enc.at[pl.ds(0, 48)], e_send.at[1])
     wait_for(enc.at[pl.ds(0, 192)], e_send.at[2])
     wait_for(enc.at[pl.ds(0, 256)], e_send.at[3])
-    arrived(hp, h_send.at[0])
-    arrived(note_in, i_send.at[0])
+    for k in range(3):
+        wait_for(hp.at[k], h_send.at[k])
+    arrived(note, i_send.at[0])
     for b in range(2):
         wait_for(de1.at[b], d_send.at[0, b])
         arrived(de2.at[b], d_send.at[1, b])
     wait_for(de3.at[pl.ds(0, 15)], d_send.at[2, 0])
-    arrived(gx, g_send.at[0])
-    wait_for(gz_in.at[pl.ds(0, 15)], g_send.at[1])
+    arrived(gx, g_send.at[1])
+    arrived(gz, g_send.at[0])
 
 
 def shards(
@@ -514,8 +536,9 @@
             pltpu.VMEM(two + (4, ROWS, HEAD_DIM), low),
             pltpu.VMEM((4, ROWS, BLOCK), low),
             pltpu.VMEM((4, ROWS, BLOCK), low),
-            pltpu.VMEM((8, 128), f32),
-            pltpu.VMEM((4, 8, 128), f32),
+            pltpu.VMEM((2, ROWS, BLOCK), low),
+            pltpu.VMEM((4, 16, 128), f32),
+            pltpu.VMEM((4, 16, 128), f32),
             pltpu.VMEM((4 * ROWS, BLOCK), f32),
             pltpu.VMEM((2, 4, 4, 16, COLS), low),
             pltpu.VMEM((2, 4, 4, 16, COLS), low),
@@ -524,8 +547,7 @@
             pltpu.VMEM((16, 16, HEAD_DIM), low),
             pltpu.VMEM((16, 16, HEAD_DIM), low),
             pltpu.VMEM((4, 8, 128), f32),
-            pltpu.VMEM((16, 8, 128), f32),
-            pltpu.VMEM((4, 4, 8, 128), f32),
+            pltpu.VMEM((4, 8, 128), f32),
             dma((11,)),
             dma((len(PIECES),)),
             dma((HEADS_HERE,)),
@@ -539,8 +561,8 @@
             dma(two),
             dma((4,)),
             dma((4,)),
-            dma((1,)),
-            dma((1,)),
+            dma((3,)),
+            dma((4,)),
             dma((1,)),
             dma((1,)),
             dma((3, 2)),

time: 165 us -> 161 us (0.976)
  Pallas kernels: 160 us -> 157 us
    pallas_call x1, Pallas kernels: 160 us -> 157 us  [shards(): pl.pallas_call(kernel, out_shape=(pltpu.VMEM((1, ROWS, BLOCK), low), pltp...]
where the time goes in v5:
time: 161 us; the launch traced here: 160 us
  Pallas kernels  157 us (98%)
  local copies, waits for them, and re-layouts  1.93 us (1%)
    pallas_call x1, Pallas kernels, shards(): pl.pallas_call(kernel, out_shape=(pltpu.VMEM((1, ROWS, BLOCK), low), pltp...  157 us

profile of v5, /device:TPU:24, one launch (start us, length us, event | category | flops | bytes accessed | tf_op | source)
XLA Modules:
  0.0 159.5 jit_solution(8237643166500584361)
XLA Ops:
  0.6 157.0 %shard_map.103 = (bf16[1,128,1024]{2,1,0:T(8,128)(2,1)S(1)}, f32[4,4096]{1,0:T(4,128)S(1)}, f32[1,1024]{1,0:T(1,128)S(1)}) custom-call(bf16[1,128,4096]{2,1,0:T(8,128)(2,1)} %x_hbm.1, bf16[1,128,4096]{2,1,0:T(8,128)(2,1)} %og_hbm.1, bf16[1,128,512]{2,1,0:T(8,128)(2,1)} %hg_hbm.1, bf16[4,4096]{1,0:T(4,128)(2,1)} %enc_ref.1, f32[1,4096]{1,0:T(1,128)} %gain_ref.1, ...), custom_call_target="tpu_custom_call" | custom-call | flops 3221225472 | bytes 4194304 | tf_op jit(solution)/shard_map/pallas_call | solution.py:509
  157.6 0.7 copy.14
  158.3 0.6 copy.16
  158.9 0.6 copy.15

commit v6 on v5

--- a/solution.py
+++ b/solution.py
@@ -45,11 +45,11 @@
 
 
 def kernel(
-    x_hbm, og_hbm, hg_hbm, enc_ref, gain_ref, wq_hbm, wk_hbm, wv_hbm,
+    x_hbm, og_hbm, hg_hbm, enc_ref, gain_hbm, wq_hbm, wk_hbm, wv_hbm,
     ig_ref, eg_ref, gg_ref,
-    wq, wkv, xv, og, hg, lines, enc64, encx, enc, hid, inv, part, part_in, kv, qb, probs, dq, dkv,
+    wq, wkv, xv, gain_ref, og, hg, lines, enc64, encx, enc, hid, inv, part, part_in, pg, pg_in, kh, qb, probs, dq, dkv,
     hp, hp_in, hp_out, note, note_in, de, de1, de1_in, de2, de2_in, de3, de3_in, gz, gx,
-    local, z_send, x_send, z_near, z_far, x_near, x_far, p_send, p_recv, k_send, k_recv,
+    local, z_send, x_send, z_near, z_far, x_near, x_far, p_send, p_recv, a_send, a_recv, k_send, k_recv,
     e_send, e_recv, h_send, h_recv, i_send, i_recv, d_send, d_recv, g_send, g_recv,
 ):
     dp = lax.axis_index("dp")
@@ -108,11 +108,12 @@
         for c, (m, h, start, rows) in enumerate(PIECES)
     ]
     x_load = pltpu.make_async_copy(x_hbm.at[0], xv, local.at[8])
-    hg_load = pltpu.make_async_copy(hg_hbm.at[0], hg, local.at[9])
+    gain_load = pltpu.make_async_copy(gain_hbm, gain_ref, local.at[7])
+    hg_load = pltpu.make_async_copy(hg_hbm.at[0], hg.at[x], local.at[9])
     og_load = pltpu.make_async_copy(
         og_hbm.at[0, :, pl.ds(pl.multiple_of(t * BLOCK, BLOCK), BLOCK)], og, local.at[10]
     )
-    for copy in loads + [x_load, hg_load, og_load]:
+    for copy in loads + [x_load, gain_load, hg_load, og_load]:
         copy.start()
 
     barrier = pltpu.get_barrier_semaphore()
@@ -191,6 +192,7 @@
 
     def norm():
         x_load.wait()
+        gain_load.wait()
         total = jnp.zeros((ROWS, 1), jnp.float32)
         for b in range(4):
             block = xv[:, b * BLOCK : (b + 1) * BLOCK].astype(jnp.float32)
@@ -210,18 +212,23 @@
         for p in range(8):
             for b in range(4):
                 part[m, h, b, pl.ds(p * 16, 16), :] = rows[p * 64 + b * 16 : p * 64 + (b + 1) * 16]
+        source, target = part.at[m, h], part_in.at[h]
+        if m == 1:
+            for b in range(4):
+                head = hg[b, :, h * HEAD_DIM : (h + 1) * HEAD_DIM]
+                pg[h, b] = dot_nt(head, part[m, h, b]).astype(jnp.bfloat16)
+            source, target = pg.at[h], pg_in.at[h]
         for k in range(1, 4):
             remote(
-                part.at[m, h, (x + k) % 4], part_in.at[m, h, x],
-                p_send.at[m, h], p_recv.at[m, h], at_x(k),
+                source.at[(x + k) % 4], target.at[x], p_send.at[m, h], p_recv.at[m, h], at_x(k)
             ).start()
 
-    def combine(m, h):
-        arrived(part_in.at[m, h], p_recv.at[m, h])
-        total = part[m, h, x].astype(jnp.float32)
-        for k in range(1, 4):
-            total += part_in[m, h, (x + k) % 4].astype(jnp.float32)
-        kv[m, h] = total.astype(jnp.bfloat16)
+    def combine(h):
+        arrived(part_in.at[h], p_recv.at[0, h])
+        total = part[0, h, x].astype(jnp.float32)
+        for k in range(1, 4):
+            total += part_in[h, (x + k) % 4].astype(jnp.float32)
+        kh[h] = total.astype(jnp.bfloat16)
 
     scale = 1.0 / math.sqrt(HEAD_DIM)
 
@@ -243,19 +250,22 @@
         qb[h] = lax.fori_loop(0, 4, add, total).astype(jnp.bfloat16)
 
     def soften(h):
-        expo = jnp.exp(dot_nt(qb[h], kv[0, h]) * scale)
+        expo = jnp.exp(dot_nt(qb[h], kh[h]) * scale)
         soft = expo / jnp.sum(expo, axis=1, keepdims=True)
         probs[h] = soft
-        head = hg[:, h * HEAD_DIM : (h + 1) * HEAD_DIM]
+        head = hg[x, :, h * HEAD_DIM : (h + 1) * HEAD_DIM]
         spread(1, h, dot_tn(soft.astype(jnp.bfloat16), head))
 
     def attend(h):
         soft = probs[h]
-        prob_grad = dot_nt(hg[:, h * HEAD_DIM : (h + 1) * HEAD_DIM], kv[1, h])
+        arrived(pg_in.at[h], p_recv.at[1, h])
+        prob_grad = pg[h, x].astype(jnp.float32)
+        for k in range(1, 4):
+            prob_grad += pg_in[h, (x + k) % 4].astype(jnp.float32)
         mean = jnp.sum(prob_grad * soft, axis=1, keepdims=True)
         score_grad = (soft * (prob_grad - mean) * scale).astype(jnp.bfloat16)
         spread(0, h, dot_tn(score_grad, qb[h]))
-        dq[h] = jnp.dot(score_grad, kv[0, h], preferred_element_type=jnp.float32).astype(
+        dq[h] = jnp.dot(score_grad, kh[h], preferred_element_type=jnp.float32).astype(
             jnp.bfloat16
         )
 
@@ -282,6 +292,9 @@
     x_first(0, 3)
     enc_x()
     norm()
+    hg_load.wait()
+    for k in range(1, 4):
+        remote(hg.at[x], hg.at[x], a_send.at[0], a_recv.at[0], at_x(k)).start()
     x_second(0, 0)
     x_second(1, 0)
 
@@ -312,23 +325,21 @@
     share(0, 0)
     queries(0)
     queries(1)
-    hg_load.wait()
+    arrived(hg, a_recv.at[0])
 
     z_second(4)
-    combine(0, 0)
+    combine(0)
     soften(0)
 
     z_second(5)
     share(0, 1)
     z_second(6)
     share(1, 0)
-    combine(0, 1)
+    combine(1)
     soften(1)
 
     share(1, 1)
-    combine(1, 0)
     attend(0)
-    combine(1, 1)
     attend(1)
 
     def hidden_block(j):
@@ -481,8 +492,9 @@
     for h in range(HEADS_HERE):
         wait_bytes(x_send.at[h], 12 * SHARD)
         for m in range(2):
-            arrived(part.at[m, h], p_send.at[m, h])
+            arrived((part.at[0, h], pg.at[h])[m], p_send.at[m, h])
             arrived(dkv.at[m, h], k_send.at[m, h])
+    arrived(hg, a_send.at[0])
     wait_for(enc64.at[pl.ds(0, 48)], e_send.at[0])
     wait_for(enc.at[pl.ds(0, 48)], e_send.at[1])
     wait_for(enc.at[pl.ds(0, 192)], e_send.at[2])
@@ -513,14 +525,15 @@
             pltpu.VMEM((4, D), f32),
             pltpu.VMEM((1, BLOCK), f32),
         ),
-        in_specs=[hbm, hbm, hbm, vmem, vmem, hbm, hbm, hbm],
+        in_specs=[hbm, hbm, hbm, vmem, hbm, hbm, hbm, hbm],
         out_specs=(vmem, vmem, vmem),
         scratch_shapes=[
             pltpu.VMEM((HEADS_HERE, D, HEAD_DIM), low),
             pltpu.VMEM(two + (BLOCK, HEAD_DIM), low),
             pltpu.VMEM((ROWS, D), low),
+            pltpu.VMEM((1, D), f32),
             pltpu.VMEM((ROWS, BLOCK), low),
-            pltpu.VMEM((ROWS, COLS), low),
+            pltpu.VMEM((4, ROWS, COLS), low),
             pltpu.VMEM((16, BLOCK), f32),
             pltpu.VMEM((64, BLOCK), low),
             pltpu.VMEM((4, 16, BLOCK), low),
@@ -528,8 +541,10 @@
             pltpu.VMEM((ROWS, D), low),
             pltpu.VMEM((ROWS, 128), f32),
             pltpu.VMEM(two + (4, ROWS, HEAD_DIM), low),
-            pltpu.VMEM(two + (4, ROWS, HEAD_DIM), low),
-            pltpu.VMEM(two + (ROWS, HEAD_DIM), low),
+            pltpu.VMEM((HEADS_HERE, 4, ROWS, HEAD_DIM), low),
+            pltpu.VMEM((HEADS_HERE, 4, ROWS, ROWS), low),
+            pltpu.VMEM((HEADS_HERE, 4, ROWS, ROWS), low),
+            pltpu.VMEM((HEADS_HERE, ROWS, HEAD_DIM), low),
             pltpu.VMEM((HEADS_HERE, ROWS, HEAD_DIM), low),
             pltpu.VMEM((HEADS_HERE, ROWS, ROWS), f32),
             pltpu.VMEM((HEADS_HERE, ROWS, HEAD_DIM), low),
@@ -557,6 +572,8 @@
             dma((4, HEADS_HERE)),
             dma(two),
             dma(two),
+            dma((1,)),
+            dma((1,)),
             dma(two),
             dma(two),
             dma((4,)),

time: 161 us -> 160 us (level); the launches traced: 160 us -> 156 us
  Pallas kernels: 157 us -> 154 us
    pallas_call x1, Pallas kernels: 157 us -> 154 us  [shards(): pl.pallas_call(kernel, out_shape=(pltpu.VMEM((1, ROWS, BLOCK), low), pltp...]
where the time goes in v6:
time: 160 us; the launch traced here: 156 us
  Pallas kernels  154 us (96%)
  local copies, waits for them, and re-layouts  1.93 us (1%)
    pallas_call x1, Pallas kernels, shards(): pl.pallas_call(kernel, out_shape=(pltpu.VMEM((1, ROWS, BLOCK), low), pltp...  154 us

profile of v6, /device:TPU:24, one launch (start us, length us, event | category | flops | bytes accessed | tf_op | source)
XLA Modules:
  0.0 156.5 jit_solution(12136121687738963421)
XLA Ops:
  0.6 153.9 %shard_map.103 = (bf16[1,128,1024]{2,1,0:T(8,128)(2,1)S(1)}, f32[4,4096]{1,0:T(4,128)S(1)}, f32[1,1024]{1,0:T(1,128)S(1)}) custom-call(bf16[1,128,4096]{2,1,0:T(8,128)(2,1)} %x_hbm.1, bf16[1,128,4096]{2,1,0:T(8,128)(2,1)} %og_hbm.1, bf16[1,128,512]{2,1,0:T(8,128)(2,1)} %hg_hbm.1, bf16[4,4096]{1,0:T(4,128)(2,1)} %enc_ref.1, f32[1,4096]{1,0:T(1,128)} %gain_hbm.1, ...), custom_call_target="tpu_custom_call" | custom-call | flops 3221225472 | bytes 4194304 | tf_op jit(solution)/shard_map/pallas_call | solution.py:521
  154.5 0.7 copy.14
  155.2 0.6 copy.16
  155.8 0.6 copy.15

commit v7 on v6

--- a/solution.py
+++ b/solution.py
@@ -322,17 +322,17 @@
     x_second(1, 3)
     x_second(1, 2)
     wait_for(enc.at[pl.ds(0, 256)], e_recv.at[3])
-    share(0, 0)
     queries(0)
     queries(1)
     arrived(hg, a_recv.at[0])
 
     z_second(4)
+    share(0, 0)
+
+    z_second(5)
+    share(0, 1)
     combine(0)
     soften(0)
-
-    z_second(5)
-    share(0, 1)
     z_second(6)
     share(1, 0)
     combine(1)
@@ -421,7 +421,7 @@
 
     for b, cols in enumerate(halves):
         wait_for(de1_in.at[b], d_recv.at[0, b])
-        for k in range(1, 4):
+        for k in (2, 1, 3):
             to = (y + k) % 4
             for s in range(4):
                 de2[b, to, s] = (

time: 160 us -> 158 us (0.988); the launches traced: 156 us -> 158 us
  no operation moved by 1% of the time
where the time goes in v7:
time: 158 us
  Pallas kernels  155 us (98%)
  local copies, waits for them, and re-layouts  1.93 us (1%)
    pallas_call x1, Pallas kernels, shards(): pl.pallas_call(kernel, out_shape=(pltpu.VMEM((1, ROWS, BLOCK), low), pltp...  155 us

profile of v7, /device:TPU:24, one launch (start us, length us, event | category | flops | bytes accessed | tf_op | source)
XLA Modules:
  0.0 157.5 jit_solution(7199361911670049940)
XLA Ops:
  0.6 155.0 %shard_map.103 = (bf16[1,128,1024]{2,1,0:T(8,128)(2,1)S(1)}, f32[4,4096]{1,0:T(4,128)S(1)}, f32[1,1024]{1,0:T(1,128)S(1)}) custom-call(bf16[1,128,4096]{2,1,0:T(8,128)(2,1)} %x_hbm.1, bf16[1,128,4096]{2,1,0:T(8,128)(2,1)} %og_hbm.1, bf16[1,128,512]{2,1,0:T(8,128)(2,1)} %hg_hbm.1, bf16[4,4096]{1,0:T(4,128)(2,1)} %enc_ref.1, f32[1,4096]{1,0:T(1,128)} %gain_hbm.1, ...), custom_call_target="tpu_custom_call" | custom-call | flops 3221225472 | bytes 4194304 | tf_op jit(solution)/shard_map/pallas_call | solution.py:521
  155.6 0.7 copy.14
  156.3 0.6 copy.16
  156.9 0.6 copy.15
